TPU v7x, 256 devices: a whole 4x4x8 slice. The times are simulated.
256 devices in a mesh: order: 16 (over z_hi, y, core), chan: 16 (over x, z_lo).
Axes of the slice: x: 4, y: 4, z: 8 (z_hi: 2, z_lo: 4; z = z_hi * 4 + z_lo), core: 2. Of those that a mesh axis runs over, the one named last changes fastest.
Arguments:
- window: int32 [1], replicated, may hold values from 0 to 712
- inputs: bfloat16 [2, 2, 8, 720, 2048], P(None, None, None, 'order', 'chan'), may hold values from -6 to 6
- out_grad: bfloat16 [2, 2, 8, 720, 2048], P(None, None, None, 'order', 'chan'), may hold values from -6 to 6
- weights: bfloat16 [2, 16384, 2048], P(None, None, 'chan'), may hold values from -0.1875 to 0.1875
Outputs:
- in_grad: float32 [2, 2, 8, 720, 2048], P(None, None, None, 'order', 'chan')
- weight_grad: float32 [2, 16384, 2048], P(None, 'order', 'chan')
Inputs may be any that keep to these rules, and one draw needn't show every extreme that they name: window[0] + 8 <= 720.
All inputs are finite; a program needn't handle non-finite values.
Results may differ from a plain program's by a relative error of at most 0.0003.
Values may be sent and summed in bfloat16 or wider, within the bound.
A program may use at most 128 MiB of HBM per device.

v0:
```python
import jax
import jax.numpy as jnp
from jax import lax
from jax.sharding import PartitionSpec as P


def complex_wgrad(left_re, left_im, right_re, right_im, form):
    wgrad_re = jnp.einsum(form, left_re, right_re, preferred_element_type=jnp.float32) + jnp.einsum(
        form, left_im, right_im, preferred_element_type=jnp.float32
    )
    wgrad_im = jnp.einsum(form, left_re, right_im, preferred_element_type=jnp.float32) - jnp.einsum(
        form, left_im, right_re, preferred_element_type=jnp.float32
    )
    return jnp.stack([wgrad_re, wgrad_im])


def complex_back(cot_re, cot_im, mix_re, mix_im):
    form = "blmo,lio->blmi"
    back_re = jnp.einsum(form, cot_re, mix_re, preferred_element_type=jnp.float32) + jnp.einsum(
        form, cot_im, mix_im, preferred_element_type=jnp.float32
    )
    back_im = jnp.einsum(form, cot_im, mix_re, preferred_element_type=jnp.float32) - jnp.einsum(
        form, cot_re, mix_im, preferred_element_type=jnp.float32
    )
    return jnp.stack([back_re, back_im])


def per_device(window, inputs, out_grad, weights):
    degree_count = inputs.shape[2]
    local_orders = inputs.shape[3]
    local_cols = out_grad.shape[4]
    channels = weights.shape[1] // degree_count
    first_order = lax.axis_index("order") * local_orders
    degrees = window[0] + jnp.arange(degree_count, dtype=jnp.int32)
    orders = first_order + jnp.arange(local_orders, dtype=jnp.int32)
    live_mask = (orders[None, :] <= degrees[:, None]).astype(jnp.bfloat16)[:, :, None]
    masked_in = inputs * live_mask
    masked_grad = out_grad * live_mask
    grad_re, grad_im = (masked_grad[0], masked_grad[1])
    mixing = weights.reshape(2, degree_count, channels, local_cols)
    partial_back = complex_back(grad_re, grad_im, mixing[0], mixing[1])
    in_grad = lax.psum_scatter(partial_back, "chan", scatter_dimension=4, tiled=True)
    column_block = lax.all_gather(masked_in, "chan", axis=4, tiled=True)
    partial_w = complex_wgrad(column_block[0], column_block[1], grad_re, grad_im, "blmi,blmo->lio")
    partial_w = partial_w.reshape(2, degree_count * channels, local_cols)
    weight_grad = lax.psum_scatter(partial_w, "order", scatter_dimension=1, tiled=True)
    return (in_grad, weight_grad)


def solution(mesh):
    placed = (
        P(),
        P(None, None, None, "order", "chan"),
        P(None, None, None, "order", "chan"),
        P(None, None, "chan"),
    )
    return jax.shard_map(
        per_device,
        mesh=mesh,
        in_specs=placed,
        out_specs=(P(None, None, None, "order", "chan"), P(None, "order", "chan")),
        check_vma=False,
    )
```

profile of v0, /device:TPU:1, one launch (start us, length us, event | category | flops | bytes accessed | tf_op | source)
XLA Modules:
  0.0 669.3 jit_solution(14023158356701046789)
XLA Ops:
  7.2 0.0 all-gather.2.cloned.1.call-start
  7.9 0.1 compare_convert_fusion
  8.0 2.0 copy_multiply_fusion
  10.0 0.0 all-gather.2.cloned.1.call-update
  10.0 0.0 reduce-scatter.3.cloned.1.call-start
  10.0 3.8 fusion.4
  13.8 1.5 fusion.3
  15.3 1.5 fusion.2
  16.7 1.5 subtract_bitcast_fusion
  18.2 4.1 add_bitcast_fusion
  22.3 9.3 %pad_maximum_fusion.1 = f32[2,2,8,45,2048]{4,3,1,2,0:T(8,128)} fusion(f32[1,2,8,45,2048]{4,3,1,2,0:T(8,128)S(1)} %subtract_bitcast_fusion, f32[1,2,8,45,2048]{4,3,1,2,0:T(8,128)} %add_bitcast_fusion), kind=kLoop, calls=%fused_computation.1 | loop fusion | flops 2949120 | bytes 23592960 | tf_op jit(solution)/shard_map/stack | solution.py:25
  31.6 0.0 reduce-scatter.3.cloned.1.call-update
  31.7 0.2 reduce-scatter.5.cloned.1.call-start
  31.9 126.7 %all-gather.2.cloned.1.call-done = bf16[2,2,8,45,2048]{4,3,1,2,0:T(8,128)(2,1)} async-done(((bf16[2,2,8,45,128]{4,3,1,2,0:T(8,128)(2,1)}), bf16[2,2,8,45,2048]{4,3,1,2,0:T(8,128)(2,1)}) %all-gather.2.cloned.1.call-update) | async-done | bytes 5898256 | tf_op jit(solution)/shard_map/all_gather | solution.py:43
  158.6 0.0 copy-start
  158.6 3.5 fusion
  162.1 0.2 copy-done
  162.3 1.5 fusion.1
  163.8 3.4 bitcast_subtract_fusion
  167.3 3.4 bitcast_add_fusion
  170.7 6.1 pad_maximum_fusion
  176.8 0.0 reduce-scatter.5.cloned.1.call-update
  176.8 260.5 %reduce-scatter.3.cloned.1.call-done = f32[2,2,8,45,128]{4,3,1,2,0:T(8,128)} async-done(((f32[2,2,8,45,2048]{4,3,1,2,0:T(8,128)}), f32[2,2,8,45,128]{4,3,1,2,0:T(8,128)}) %reduce-scatter.3.cloned.1.call-update) | async-done | bytes 737296 | tf_op jit(solution)/shard_map/reduce_scatter | solution.py:42
  437.3 2.4 copy.8
  439.7 223.1 %reduce-scatter.5.cloned.1.call-done = f32[2,1024,128]{2,1,0:T(8,128)} async-done(((f32[2,16384,128]{2,1,0:T(8,128)}), f32[2,1024,128]{2,1,0:T(8,128)}) %reduce-scatter.5.cloned.1.call-update) | async-done | bytes 1048592 | tf_op jit(solution)/shard_map/reduce_scatter | solution.py:46
  (2 shorter events, 0.0 us)
Async XLA Ops:
  7.2 151.4 %all-gather.2.cloned.1.call-start = ((), (), s32[]{:S(2)}) async-start(), calls=%async_computation.3 | async-start | bytes 6684672 | tf_op jit(solution)/shard_map/all_gather | solution.py:43
  10.0 427.3 %reduce-scatter.3.cloned.1.call-start = ((), (), s32[]{:S(2)}) async-start(), calls=%async_computation.2 | async-start | bytes 13369344 | tf_op jit(solution)/shard_map/reduce_scatter | solution.py:42
  31.7 631.1 %reduce-scatter.5.cloned.1.call-start = ((), (), s32[]{:S(2)}) async-start(), calls=%async_computation.4 | async-start | bytes 17825792 | tf_op jit(solution)/shard_map/reduce_scatter | solution.py:46
  158.6 3.7 copy-start
Sparse Core Ops, SparseCore 0:
  10.3 148.2 all-gather.1
  161.2 276.0 reduce-scatter.2
  442.5 220.2 reduce-scatter.4
where the time goes:
time: 670 us; the launch traced here: 669 us
  waiting for transfers between devices  610 us (91%)
  matrix products  20.4 us (3%)
  other arithmetic  17.5 us (3%)
  between operations  14.4 us (2%)
    reduce_scatter x1, waiting for transfers between devices, per_device(): lax.psum_scatter(partial_back, 'chan', scatter_dimension=4, tiled=True)  260 us
    reduce_scatter x1, waiting for transfers between devices, per_device(): lax.psum_scatter(partial_w, 'order', scatter_dimension=1, tiled=True)  223 us
    all_gather x1, waiting for transfers between devices, per_device(): column_block = lax.all_gather(masked_in, 'chan', axis=4, tiled=True)  127 us
  transfers between devices with their start and end apart: 3, of which 3 were waited for; matrix products, arithmetic and copies ran while one was open for 6% of the time, Pallas kernels for 0%

commit v1 on v0

v1 whole, which is shorter than its diff:
```python
import functools

import jax
import jax.numpy as jnp
from jax import lax
from jax.experimental import pallas as pl
from jax.experimental.pallas import tpu as pltpu
from jax.sharding import PartitionSpec as P

MESH = pl.DeviceIdType.MESH
BF16, F32 = jnp.bfloat16, jnp.float32

NX, NY, NZ = 4, 4, 4
NB = 8


def coords():
    order, chan = lax.axis_index("order"), lax.axis_index("chan")
    return order // 8, (order // 2) % 4, order % 2, chan // 4, chan % 4


def lanes(block):
    return pl.ds(pl.multiple_of(block * 128, 128), 128)


def kernel(
    rows, x_ref, g_ref, w_ref, back_ref, wgrad_ref,
    xz, gx, gz, wt, acc, pair, part, heap, fin, ret, wg,
    xa_s, xa_r, ga_s, ga_r, gi_s, gi_r, w_s, w_r, w_loc,
    xr_s, xl_s, xz_r, gr_s, gl_s, gz_r, gx_s, gx_r,
    pair_s, pair_r, wo_s, wo_r, rs_s, rs_r, rt_s, rt_r, out_s,
):
    zh, y, k, x, zl = coords()
    z = zh * 4 + zl
    half = rows // 2
    me = y * 2 + k

    def dev(zh_, y_, k_, x_, zl_):
        return (zh_ * 8 + y_ * 2 + k_, x_ * 4 + zl_)

    def at_z(z_):
        return dev(z_ // 4, y, k, x, z_ % 4)

    def greet(device):
        pl.semaphore_signal(pltpu.get_barrier_semaphore(), inc=1, device_id=device, device_id_type=MESH)

    def greet_order(t, _):
        other = (zh * 8 + me + t) % 16
        greet((other, x * 4 + zl))
        return 0

    lax.fori_loop(1, 16, greet_order, 0)
    for d in (1, 2, 3, 5, 6, 7):
        greet(at_z((z + d) % 8))
    for d in (1, 2, 3):
        for other in (0, 1):
            greet(dev(zh, y, other, (x + d) % 4, zl))
    pl.semaphore_wait(pltpu.get_barrier_semaphore(), 15 + 6 + 6)

    def remote(src, dst, send, recv, device):
        return pltpu.make_async_remote_copy(
            src_ref=src, dst_ref=dst, send_sem=send, recv_sem=recv, device_id=device, device_id_type=MESH
        )

    def blk(buf, b, lane):
        return buf.at[b, :, lanes(lane)]

    def to_weight(src, buf, lane, send, recv, t):
        e = (zh * 4 + y + t) % 8
        remote(src.at[e], blk(buf, me, lane), send.at[e], recv.at[me], dev(e // 4, e % 4, zh, x, zl)).start()

    def own_weight(src, buf, lane, recv, e):
        pltpu.make_async_copy(src.at[e], blk(buf, me, lane), recv.at[me]).start()

    def weight_out(src, buf, lane, send, recv):
        mine = zh == k

        @pl.when(mine)
        def _():
            own_weight(src, buf, lane, recv, zh * 4 + y)

        @pl.when(jnp.logical_not(mine))
        def _():
            to_weight(src, buf, lane, send, recv, 0)

        def step(t, _):
            to_weight(src, buf, lane, send, recv, t)
            return 0

        lax.fori_loop(1, 8, step, 0)

    def to_input(t):
        j = (me + t) % 8
        y_, k_ = j // 2, j % 2
        return remote(g_ref.at[4 * k_ + y_], blk(gz, me, zl), gi_s.at[j], gi_r.at[me], dev(zh, y_, k_, x, zl))

    weight_out(x_ref, xz, zl, xa_s, xa_r)
    weight_out(g_ref, gx, x, ga_s, ga_r)

    degree = 4 * k + y
    w_loc_copy = pltpu.make_async_copy(w_ref.at[:, degree, :, zl], wt.at[:, :, :, lanes(zl)], w_loc)
    w_loc_copy.start()
    w_copies = []
    for i, (d, part_of) in enumerate(((1, (0, 2)), (7, (0, 2)), (2, (0, 1)), (6, (1, 1)))):
        to = (z + d) % 8
        reim = pl.ds(*part_of)
        w_copies.append(
            remote(w_ref.at[reim, degree, :, to % 4], wt.at[reim, :, :, lanes(zl)], w_s.at[i], w_r.at[i], at_z(to))
        )
        w_copies[-1].start()

    def gi_step(t, _):
        to_input(t).start()
        return 0

    lax.fori_loop(1, 8, gi_step, 0)
    pltpu.make_async_copy(g_ref.at[degree], blk(gz, me, zl), gi_r.at[me]).start()

    def right(buf, o, b, send, recv):
        return remote(blk(buf, b, o), blk(buf, b, o), send.at[o, b], recv.at[o, b], dev(zh, y, k, x, (zl + 1) % 4))

    def left(buf, o, b, send, recv):
        return remote(blk(buf, b, o), blk(buf, b, o), send.at[o, b], recv.at[o, b], dev(zh, y, k, x, (zl + 3) % 4))

    def own_line(buf, b, s_r, s_l, recv):
        @pl.when(zl < 3)
        def _():
            right(buf, zl, b, s_r, recv).start()

        @pl.when(zl > 0)
        def _():
            left(buf, zl, b, s_l, recv).start()

    def pass_line(buf, b, d, s_r, s_l, recv):
        @pl.when(zl >= d)
        def _():
            o = zl - d
            right(buf, o, b, s_r, recv).wait_recv()

            @pl.when(zl < 3)
            def _():
                right(buf, o, b, s_r, recv).start()

        @pl.when(zl + d <= 3)
        def _():
            o = zl + d
            left(buf, o, b, s_l, recv).wait_recv()

            @pl.when(zl > 0)
            def _():
                left(buf, o, b, s_l, recv).start()

    def drain_line(buf, b, s_r, s_l, recv):
        for d in range(3):
            @pl.when((zl >= d) & (zl < 3))
            def _():
                right(buf, zl - d, b, s_r, recv).wait_send()

            @pl.when((zl + d <= 3) & (zl > 0))
            def _():
                left(buf, zl + d, b, s_l, recv).wait_send()

    def ring(d, b):
        return remote(blk(gx, b, x), blk(gx, b, x), gx_s.at[d, b], gx_r.at[d, b], dev(zh, y, k, (x + d) % 4, zl))

    def first(b, _):
        pltpu.make_async_copy(x_ref.at[0], blk(xz, b, zl), xa_r.at[b]).wait()
        own_line(xz, b, xr_s, xl_s, xz_r)
        pltpu.make_async_copy(g_ref.at[0], blk(gx, b, x), ga_r.at[b]).wait()
        for d in (1, 3, 2):
            ring(d, b).start()
        return 0

    lax.fori_loop(0, NB, first, 0)

    def second(b, _):
        pltpu.make_async_copy(g_ref.at[0], blk(gz, b, zl), gi_r.at[b]).wait()
        own_line(gz, b, gr_s, gl_s, gz_r)
        return 0

    lax.fori_loop(0, NB, second, 0)

    def pass_x(d):
        def step(b, _):
            pass_line(xz, b, d, xr_s, xl_s, xz_r)
            return 0

        lax.fori_loop(0, NB, step, 0)

    def pass_g(d):
        def step(b, _):
            pass_line(gz, b, d, gr_s, gl_s, gz_r)
            return 0

        lax.fori_loop(0, NB, step, 0)

    pass_x(1)
    pass_g(1)
    pass_x(2)

    acc[...] = jnp.zeros_like(acc)

    def wgrad_step(c, _):
        for j in range(2):
            b = 2 * c + j
            pass_line(xz, b, 3, xr_s, xl_s, xz_r)
            for d in (1, 2, 3):
                remote(
                    blk(gx, b, x), blk(gx, b, (x + 4 - d) % 4), gx_s.at[d, b], gx_r.at[d, b],
                    dev(zh, y, k, (x + d) % 4, zl),
                ).wait_recv()
        left_ = xz[pl.ds(2 * c, 2)].reshape(2 * rows, 512)
        right_ = gx[pl.ds(2 * c, 2)]
        turned = jnp.concatenate([right_[:, half:], -right_[:, :half]], axis=1).reshape(2 * rows, 512)
        right_ = right_.reshape(2 * rows, 512)
        over_rows = (((0,), (0,)), ((), ()))
        acc[0] += lax.dot_general(left_, right_, over_rows, preferred_element_type=F32)
        acc[1] += lax.dot_general(left_, turned, over_rows, preferred_element_type=F32)
        return 0

    lax.fori_loop(0, NB // 2, wgrad_step, 0)

    swap = remote(acc.at[1 - k], pair, pair_s, pair_r, dev(zh, y, 1 - k, x, zl))
    swap.start()
    pass_g(2)
    swap.wait_recv()
    acc[k] = acc[k] + pair[...]

    def wgrad_to(d):
        return remote(
            acc.at[k, :, lanes((x + d) % 4)],
            wg.at[k, pl.ds(pl.multiple_of((x % 2) * 512, 512), 512)],
            wo_s.at[d], wo_r.at[x % 2, k], dev(zh, y, x // 2, (x + d) % 4, zl),
        )

    for d in (1, 3, 2):
        wgrad_to(d).start()

    @pl.when(k == x // 2)
    def _():
        pltpu.make_async_copy(
            acc.at[k, :, lanes(x)], wg.at[k, pl.ds(pl.multiple_of((x % 2) * 512, 512), 512)], wo_r.at[x % 2, k]
        ).start()

    @pl.when(k != x // 2)
    def _():
        wgrad_to(0).start()

    w_loc_copy.wait()
    for copy in w_copies:
        copy.wait_recv()

    def scatter(d, c):
        x_ = (x + d) % 4
        return remote(
            part.at[x_, pl.ds(2 * c, 2)], heap.at[d - 1, pl.ds(2 * c, 2)], rs_s.at[d - 1, c], rs_r.at[d - 1, c],
            dev(zh, y, k, x_, zl),
        )

    def home(b):
        y_, k_ = b // 2, b % 2
        return remote(fin.at[b], ret.at[degree], rt_s.at[b], rt_r.at[degree], dev(zh, y_, k_, x, zl))

    def reduce_step(c):
        for d in (1, 2, 3):
            scatter(d, c).wait_recv()
        for j in range(2):
            b = 2 * c + j
            fin[b] = (part[x, b] + heap[0, b]) + (heap[1, b] + heap[2, b])

            @pl.when(b == me)
            def _():
                pltpu.make_async_copy(fin.at[b], ret.at[degree], rt_r.at[degree]).start()

            @pl.when(b != me)
            def _():
                home(b).start()

    def back_step(c, _):
        for j in range(2):
            pass_line(gz, 2 * c + j, 3, gr_s, gl_s, gz_r)
        cot = gz[pl.ds(2 * c, 2)].reshape(2 * rows, 512)
        over_lanes = (((1,), (1,)), ((), ()))
        by_re = lax.dot_general(cot, wt[0].reshape(512, 512), over_lanes, preferred_element_type=F32)
        by_im = lax.dot_general(cot, wt[1].reshape(512, 512), over_lanes, preferred_element_type=F32)
        for j in range(2):
            lo, mid, hi = j * rows, j * rows + half, (j + 1) * rows
            back_re = by_re[lo:mid] + by_im[mid:hi]
            back_im = by_re[mid:hi] - by_im[lo:mid]
            for x_ in range(NX):
                part[x_, 2 * c + j, 0:half] = back_re[:, x_ * 128 : (x_ + 1) * 128]
                part[x_, 2 * c + j, half:rows] = back_im[:, x_ * 128 : (x_ + 1) * 128]
        for d in (1, 3, 2):
            scatter(d, c).start()

        @pl.when(c > 0)
        def _():
            reduce_step(c - 1)

        return 0

    lax.fori_loop(0, NB // 2, back_step, 0)
    reduce_step(NB // 2 - 1)

    for r in range(2):
        for k_ in range(2):
            pltpu.make_async_copy(
                acc.at[0, :, pl.ds(0, 128)], wg.at[k_, pl.ds(r * 512, 512)], wo_r.at[r, k_]
            ).wait()
    wg_out = pltpu.make_async_copy(wg, wgrad_ref, out_s.at[0])
    wg_out.start()

    def returned(l, _):
        pltpu.make_async_copy(fin.at[0], ret.at[l], rt_r.at[l]).wait()
        return 0

    lax.fori_loop(0, NB, returned, 0)
    back_out = pltpu.make_async_copy(ret, back_ref, out_s.at[1])
    back_out.start()

    def drain(b, _):
        drain_line(xz, b, xr_s, xl_s, xz_r)
        drain_line(gz, b, gr_s, gl_s, gz_r)
        for d in (1, 2, 3):
            ring(d, b).wait_send()

        @pl.when(jnp.logical_or(zh != k, b != zh * 4 + y))
        def _():
            pltpu.make_async_copy(x_ref.at[b], blk(xz, 0, zl), xa_s.at[b]).wait()
            pltpu.make_async_copy(g_ref.at[b], blk(gx, 0, x), ga_s.at[b]).wait()

        @pl.when(b != me)
        def _():
            pltpu.make_async_copy(g_ref.at[0], blk(gz, 0, zl), gi_s.at[b]).wait()
            home(b).wait_send()

        return 0

    lax.fori_loop(0, NB, drain, 0)

    def drain_scatter(c, _):
        for d in (1, 2, 3):
            scatter(d, c).wait_send()
        return 0

    lax.fori_loop(0, NB // 2, drain_scatter, 0)
    for copy in w_copies:
        copy.wait_send()
    swap.wait_send()
    for d in (1, 2, 3):
        wgrad_to(d).wait_send()

    @pl.when(k != x // 2)
    def _():
        wgrad_to(0).wait_send()

    wg_out.wait()
    back_out.wait()


def per_device(window, inputs, out_grad, weights):
    _, samples, degrees, orders, width = inputs.shape
    first_order = lax.axis_index("order") * orders
    degree = window[0] + jnp.arange(degrees, dtype=jnp.int32)
    order = first_order + jnp.arange(orders, dtype=jnp.int32)
    live = (order[None, :] <= degree[:, None]).astype(BF16)[:, :, None]
    real = samples * orders
    half = -(-real // 16) * 16
    rows = 2 * half

    def by_degree(a):
        a = (a * live).transpose(2, 0, 1, 3, 4).reshape(degrees, 2, real, width)
        return jnp.pad(a, ((0, 0), (0, 0), (0, half - real), (0, 0))).reshape(degrees, rows, width)

    dma, vmem = pltpu.SemaphoreType.DMA, pltpu.VMEM
    back, wgrad = pl.pallas_call(
        functools.partial(kernel, rows),
        name="mix_back",
        out_shape=(
            jax.ShapeDtypeStruct((degrees, rows, width), F32),
            jax.ShapeDtypeStruct((2, 1024, width), F32),
        ),
        in_specs=[
            pl.BlockSpec(memory_space=pltpu.VMEM),
            pl.BlockSpec(memory_space=pltpu.VMEM),
            pl.BlockSpec(memory_space=pl.ANY),
        ],
        out_specs=(pl.BlockSpec(memory_space=pl.ANY), pl.BlockSpec(memory_space=pl.ANY)),
        scratch_shapes=[
            vmem((NB, rows, 512), BF16),
            vmem((NB, rows, 512), BF16),
            vmem((NB, rows, 512), BF16),
            vmem((2, 4, 128, 512), BF16),
            vmem((2, 512, 512), F32),
            vmem((512, 512), F32),
            vmem((NX, NB, rows, 128), F32),
            vmem((3, NB, rows, 128), F32),
            vmem((NB, rows, 128), F32),
            vmem((NB, rows, 128), F32),
            vmem((2, 1024, 128), F32),
            dma((8,)), dma((8,)), dma((8,)), dma((8,)), dma((8,)), dma((8,)), dma((4,)), dma((4,)), dma(()),
            dma((4, 8)), dma((4, 8)), dma((4, 8)), dma((4, 8)), dma((4, 8)), dma((4, 8)), dma((4, 8)), dma((4, 8)),
            dma(()), dma(()), dma((4,)), dma((2, 2)), dma((3, 4)), dma((3, 4)), dma((8,)), dma((8,)), dma((2,)),
        ],
        compiler_params=pltpu.CompilerParams(
            collective_id=0, has_side_effects=True, vmem_limit_bytes=44 * 2**20
        ),
    )(by_degree(inputs), by_degree(out_grad), weights.reshape(2, degrees, 4, 4, 128, width))
    back = back.reshape(degrees, 2, half, width)[:, :, :real].reshape(degrees, 2, samples, orders, width)
    return back.transpose(1, 2, 0, 3, 4), wgrad


def solution(mesh):
    placed = (
        P(),
        P(None, None, None, "order", "chan"),
        P(None, None, None, "order", "chan"),
        P(None, None, "chan"),
    )
    return jax.shard_map(
        per_device,
        mesh=mesh,
        in_specs=placed,
        out_specs=(P(None, None, None, "order", "chan"), P(None, "order", "chan")),
        check_vma=False,
    )
```

time: 670 us -> 153 us (0.23)
  waiting for transfers between devices: 610 us -> 0 us
  Pallas kernels: 0 us -> 148 us
  matrix products: 20.4 us -> 0 us
  other arithmetic: 17.5 us -> 1.3 us
  between operations: 14.4 us -> 1.34 us
    reduce_scatter x2 -> x0, waiting for transfers between devices: 484 us -> none  [the longest x1 260 us: per_device(): lax.psum_scatter(partial_back, 'chan', scatter_dimension=4, tiled=True)]
    pallas_call x0 -> x1, Pallas kernels: none -> 148 us  [per_device(): pl.pallas_call(functools.partial(kernel, rows), name='mix_back', out_shap...]
    all_gather x1 -> x0, waiting for transfers between devices: 127 us -> none  [per_device(): column_block = lax.all_gather(masked_in, 'chan', axis=4, tiled=True)]
    dot_general x8 -> x0, matrix products: 20.4 us -> none  [the longest x1 4.12 us: complex_back(): jnp.einsum(form, cot_im, mix_im, preferred_element_type=jnp.float32)]
    another operation x2 -> x0, other arithmetic: 15.4 us -> none  [the longest x1 9.34 us: complex_back(): return jnp.stack([back_re, back_im])]
  transfers between devices with their start and end apart: 3 -> 0, of which waited for: 3 -> 0; matrix products, arithmetic and copies ran while one was open for 6% -> 0% of each run, Pallas kernels for 0% -> 0%
where the time goes in v1:
time: 153 us
  Pallas kernels  148 us (97%)
  local copies, waits for them, and re-layouts  2.56 us (2%)
    pallas_call x1, Pallas kernels, per_device(): pl.pallas_call(functools.partial(kernel, rows), name='mix_back', out_shap...  148 us

profile of v1, /device:TPU:1, one launch (start us, length us, event | category | flops | bytes accessed | tf_op | source)
XLA Modules:
  0.0 152.8 jit_solution(16820282597361978953)
XLA Ops:
  1.3 0.1 compare_convert_fusion
  1.4 0.1 copy.9
  1.5 1.2 broadcast_multiply_fusion
  2.7 0.1 copy.10
  2.8 0.1 copy.11
  2.9 147.6 %mix_back.1 = (f32[8,192,128]{2,1,0:T(8,128)S(1)}, f32[2,1024,128]{2,1,0:T(8,128)S(1)}) custom-call(bf16[8,192,128]{2,1,0:T(8,128)(2,1)S(1)} %bitcast.16, bf16[8,192,128]{2,1,0:T(8,128)(2,1)S(1)} %bitcast.17, bf16[2,8,4,4,128,128]{5,4,3,2,1,0:T(8,128)(2,1)} %bitcast.19), custom_call_target="tpu_custom_call" | custom-call | tf_op jit(solution)/shard_map/mix_back/pallas_call | solution.py:376
  150.5 1.3 copy.12
  151.8 1.0 copy.15
  (4 shorter events, 0.1 us)

commit v2 on v1

--- a/solution.py
+++ b/solution.py
@@ -25,10 +25,10 @@
 
 def kernel(
     rows, x_ref, g_ref, w_ref, back_ref, wgrad_ref,
-    xz, gx, gz, wt, acc, pair, part, heap, fin, ret, wg,
+    xz, gx, gp, gz, wt, acc, pair, part, relay, heap, fin, ret, wg,
     xa_s, xa_r, ga_s, ga_r, gi_s, gi_r, w_s, w_r, w_loc,
     xr_s, xl_s, xz_r, gr_s, gl_s, gz_r, gx_s, gx_r,
-    pair_s, pair_r, wo_s, wo_r, rs_s, rs_r, rt_s, rt_r, out_s,
+    pair_s, pair_r, wo_s, wo_r, far_s, far_r, rs_s, rs_r, rt_s, rt_r, out_s,
 ):
     zh, y, k, x, zl = coords()
     z = zh * 4 + zl
@@ -94,10 +94,15 @@
         y_, k_ = j // 2, j % 2
         return remote(g_ref.at[4 * k_ + y_], blk(gz, me, zl), gi_s.at[j], gi_r.at[me], dev(zh, y_, k_, x, zl))
 
-    weight_out(x_ref, xz, zl, xa_s, xa_r)
+    def gi_step(t, _):
+        to_input(t).start()
+        return 0
+
+    lax.fori_loop(1, 8, gi_step, 0)
+    degree = 4 * k + y
+    pltpu.make_async_copy(g_ref.at[degree], blk(gz, me, zl), gi_r.at[me]).start()
     weight_out(g_ref, gx, x, ga_s, ga_r)
 
-    degree = 4 * k + y
     w_loc_copy = pltpu.make_async_copy(w_ref.at[:, degree, :, zl], wt.at[:, :, :, lanes(zl)], w_loc)
     w_loc_copy.start()
     w_copies = []
@@ -109,13 +114,6 @@
         )
         w_copies[-1].start()
 
-    def gi_step(t, _):
-        to_input(t).start()
-        return 0
-
-    lax.fori_loop(1, 8, gi_step, 0)
-    pltpu.make_async_copy(g_ref.at[degree], blk(gz, me, zl), gi_r.at[me]).start()
-
     def right(buf, o, b, send, recv):
         return remote(blk(buf, b, o), blk(buf, b, o), send.at[o, b], recv.at[o, b], dev(zh, y, k, x, (zl + 1) % 4))
 
@@ -160,113 +158,94 @@
             def _():
                 left(buf, zl + d, b, s_l, recv).wait_send()
 
-    def ring(d, b):
-        return remote(blk(gx, b, x), blk(gx, b, x), gx_s.at[d, b], gx_r.at[d, b], dev(zh, y, k, (x + d) % 4, zl))
-
-    def first(b, _):
-        pltpu.make_async_copy(x_ref.at[0], blk(xz, b, zl), xa_r.at[b]).wait()
-        own_line(xz, b, xr_s, xl_s, xz_r)
-        pltpu.make_async_copy(g_ref.at[0], blk(gx, b, x), ga_r.at[b]).wait()
-        for d in (1, 3, 2):
-            ring(d, b).start()
-        return 0
-
-    lax.fori_loop(0, NB, first, 0)
-
-    def second(b, _):
-        pltpu.make_async_copy(g_ref.at[0], blk(gz, b, zl), gi_r.at[b]).wait()
-        own_line(gz, b, gr_s, gl_s, gz_r)
-        return 0
-
-    lax.fori_loop(0, NB, second, 0)
-
-    def pass_x(d):
-        def step(b, _):
+    def ring_right(o, b):
+        return remote(blk(gx, b, o), blk(gx, b, o), gx_s.at[0, b], gx_r.at[0, b], dev(zh, y, k, (x + 1) % 4, zl))
+
+    def ring_left(o, b):
+        return remote(blk(gx, b, o), blk(gx, b, o), gx_s.at[1, b], gx_r.at[1, b], dev(zh, y, k, (x + 3) % 4, zl))
+
+    def ring_far(to_right, b):
+        o, to = ((x + 3) % 4, (x + 1) % 4) if to_right else ((x + 1) % 4, (x + 3) % 4)
+        return remote(blk(gx, b, o), blk(gx, b, o), gx_s.at[2, b], gx_r.at[2, b], dev(zh, y, k, to, zl))
+
+    def pair_of(c):
+        return (2 * c, 2 * c + 1)
+
+    def g_own(c):
+        for b in pair_of(c):
+            pltpu.make_async_copy(g_ref.at[0], blk(gz, b, zl), gi_r.at[b]).wait()
+            own_line(gz, b, gr_s, gl_s, gz_r)
+
+    def g_pass(c, d):
+        for b in pair_of(c):
+            pass_line(gz, b, d, gr_s, gl_s, gz_r)
+
+    def x_own(c):
+        for b in pair_of(c):
+            pltpu.make_async_copy(x_ref.at[0], blk(xz, b, zl), xa_r.at[b]).wait()
+            own_line(xz, b, xr_s, xl_s, xz_r)
+
+    def x_pass(c, d):
+        for b in pair_of(c):
             pass_line(xz, b, d, xr_s, xl_s, xz_r)
-            return 0
-
-        lax.fori_loop(0, NB, step, 0)
-
-    def pass_g(d):
-        def step(b, _):
-            pass_line(gz, b, d, gr_s, gl_s, gz_r)
-            return 0
-
-        lax.fori_loop(0, NB, step, 0)
-
-    pass_x(1)
-    pass_g(1)
-    pass_x(2)
-
-    acc[...] = jnp.zeros_like(acc)
-
-    def wgrad_step(c, _):
-        for j in range(2):
-            b = 2 * c + j
-            pass_line(xz, b, 3, xr_s, xl_s, xz_r)
-            for d in (1, 2, 3):
-                remote(
-                    blk(gx, b, x), blk(gx, b, (x + 4 - d) % 4), gx_s.at[d, b], gx_r.at[d, b],
-                    dev(zh, y, k, (x + d) % 4, zl),
-                ).wait_recv()
-        left_ = xz[pl.ds(2 * c, 2)].reshape(2 * rows, 512)
-        right_ = gx[pl.ds(2 * c, 2)]
-        turned = jnp.concatenate([right_[:, half:], -right_[:, :half]], axis=1).reshape(2 * rows, 512)
-        right_ = right_.reshape(2 * rows, 512)
-        over_rows = (((0,), (0,)), ((), ()))
-        acc[0] += lax.dot_general(left_, right_, over_rows, preferred_element_type=F32)
-        acc[1] += lax.dot_general(left_, turned, over_rows, preferred_element_type=F32)
-        return 0
-
-    lax.fori_loop(0, NB // 2, wgrad_step, 0)
-
-    swap = remote(acc.at[1 - k], pair, pair_s, pair_r, dev(zh, y, 1 - k, x, zl))
-    swap.start()
-    pass_g(2)
-    swap.wait_recv()
-    acc[k] = acc[k] + pair[...]
-
-    def wgrad_to(d):
+
+    def ring_own(c):
+        for b in pair_of(c):
+            pltpu.make_async_copy(g_ref.at[0], blk(gx, b, x), ga_r.at[b]).wait()
+            ring_right(x, b).start()
+            ring_left(x, b).start()
+
+    def ring_pass(c):
+        even, odd = pair_of(c)
+        for b in (even, odd):
+            ring_right((x + 3) % 4, b).wait_recv()
+            ring_left((x + 1) % 4, b).wait_recv()
+        ring_far(True, even).start()
+        ring_far(False, odd).start()
+
+    def ring_end(c):
+        even, odd = pair_of(c)
+        ring_far(True, even).wait_recv()
+        ring_far(False, odd).wait_recv()
+        cot = gx[pl.ds(2 * c, 2)]
+        gp[pl.ds(2 * c, 2), 0:half] = cot[:, half:]
+        gp[pl.ds(2 * c, 2), half:rows] = -cot[:, :half]
+
+    def far(way, c):
+        x_ = (x + 2) % 4
+        at = pl.ds(0, half) if way == 0 else pl.ds(half, half)
         return remote(
-            acc.at[k, :, lanes((x + d) % 4)],
-            wg.at[k, pl.ds(pl.multiple_of((x % 2) * 512, 512), 512)],
-            wo_s.at[d], wo_r.at[x % 2, k], dev(zh, y, x // 2, (x + d) % 4, zl),
+            part.at[x_, pl.ds(2 * c, 2), at], relay.at[way, pl.ds(2 * c, 2)], far_s.at[way, c], far_r.at[way, c],
+            dev(zh, y, k, (x + 1 + 2 * way) % 4, zl),
         )
 
-    for d in (1, 3, 2):
-        wgrad_to(d).start()
-
-    @pl.when(k == x // 2)
-    def _():
-        pltpu.make_async_copy(
-            acc.at[k, :, lanes(x)], wg.at[k, pl.ds(pl.multiple_of((x % 2) * 512, 512), 512)], wo_r.at[x % 2, k]
-        ).start()
-
-    @pl.when(k != x // 2)
-    def _():
-        wgrad_to(0).start()
-
-    w_loc_copy.wait()
-    for copy in w_copies:
-        copy.wait_recv()
-
-    def scatter(d, c):
-        x_ = (x + d) % 4
+    def near(way, c):
+        x_ = (x + 1 + 2 * way) % 4
         return remote(
-            part.at[x_, pl.ds(2 * c, 2)], heap.at[d - 1, pl.ds(2 * c, 2)], rs_s.at[d - 1, c], rs_r.at[d - 1, c],
+            part.at[x_, pl.ds(2 * c, 2)], heap.at[way, pl.ds(2 * c, 2)], rs_s.at[way, c], rs_r.at[way, c],
             dev(zh, y, k, x_, zl),
         )
+
+    def back_relay(c):
+        for way in (0, 1):
+            far(way, c).wait_recv()
+            x_ = (x + 1 + 2 * way) % 4
+            for b in pair_of(c):
+                if way == 0:
+                    part[x_, b, 0:half] = part[x_, b, 0:half] + relay[way, b]
+                else:
+                    part[x_, b, half:rows] = part[x_, b, half:rows] + relay[way, b]
+            near(way, c).start()
 
     def home(b):
         y_, k_ = b // 2, b % 2
         return remote(fin.at[b], ret.at[degree], rt_s.at[b], rt_r.at[degree], dev(zh, y_, k_, x, zl))
 
-    def reduce_step(c):
-        for d in (1, 2, 3):
-            scatter(d, c).wait_recv()
-        for j in range(2):
-            b = 2 * c + j
-            fin[b] = (part[x, b] + heap[0, b]) + (heap[1, b] + heap[2, b])
+    def back_reduce(c):
+        for way in (0, 1):
+            near(way, c).wait_recv()
+        for b in pair_of(c):
+            fin[b] = part[x, b] + (heap[0, b] + heap[1, b])
 
             @pl.when(b == me)
             def _():
@@ -276,9 +255,7 @@
             def _():
                 home(b).start()
 
-    def back_step(c, _):
-        for j in range(2):
-            pass_line(gz, 2 * c + j, 3, gr_s, gl_s, gz_r)
+    def back_product(c):
         cot = gz[pl.ds(2 * c, 2)].reshape(2 * rows, 512)
         over_lanes = (((1,), (1,)), ((), ()))
         by_re = lax.dot_general(cot, wt[0].reshape(512, 512), over_lanes, preferred_element_type=F32)
@@ -290,25 +267,106 @@
             for x_ in range(NX):
                 part[x_, 2 * c + j, 0:half] = back_re[:, x_ * 128 : (x_ + 1) * 128]
                 part[x_, 2 * c + j, half:rows] = back_im[:, x_ * 128 : (x_ + 1) * 128]
+        for way in (0, 1):
+            far(way, c).start()
+
+    def when_chunk(c, work):
+        @pl.when((c >= 0) & (c < 4))
+        def _():
+            work(c)
+
+    def pipeline(s, _):
+        when_chunk(s, g_own)
+        when_chunk(s - 1, lambda c: g_pass(c, 1))
+        when_chunk(s - 1, ring_own)
+        when_chunk(s - 2, lambda c: g_pass(c, 2))
+
+        @pl.when(s == 3)
+        def _():
+            weight_out(x_ref, xz, zl, xa_s, xa_r)
+            w_loc_copy.wait()
+            for copy in w_copies:
+                copy.wait_recv()
+
+        def product(c):
+            g_pass(c, 3)
+            back_product(c)
+
+        when_chunk(s - 3, product)
+        when_chunk(s - 2, ring_pass)
+        when_chunk(s - 4, back_relay)
+        when_chunk(s - 5, x_own)
+        when_chunk(s - 5, back_reduce)
+        when_chunk(s - 6, lambda c: x_pass(c, 1))
+        when_chunk(s - 6, ring_end)
+        when_chunk(s - 7, lambda c: x_pass(c, 2))
+        return 0
+
+    lax.fori_loop(0, 11, pipeline, 0)
+
+    order_of = jnp.where(zl == 0, 0o3210, jnp.where(zl == 1, 0o3201, jnp.where(zl == 2, 0o0312, 0o0123)))
+
+    def nth(t):
+        return (order_of // jnp.where(t == 0, 1, jnp.where(t == 1, 8, jnp.where(t == 2, 64, 512)))) % 8
+
+    def swap(o):
+        return remote(acc.at[1 - k, o], pair.at[o], pair_s.at[o], pair_r.at[o], dev(zh, y, 1 - k, x, zl))
+
+    def owner_rows(o):
+        return pl.ds(pl.multiple_of((x % 2) * 512 + o * 128, 128), 128)
+
+    def wgrad_to(d, o):
+        return remote(
+            acc.at[k, o, :, lanes((x + d) % 4)], wg.at[k, owner_rows(o)],
+            wo_s.at[d, o], wo_r.at[x % 2, k, o], dev(zh, y, x // 2, (x + d) % 4, zl),
+        )
+
+    def wgrad_product(t):
+        o = nth(t)
+
+        @pl.when(t == 3)
+        def _():
+            def last(b, _):
+                pass_line(xz, b, 3, xr_s, xl_s, xz_r)
+                return 0
+
+            lax.fori_loop(0, NB, last, 0)
+
+        left_ = xz[:, :, lanes(o)].reshape(NB * rows, 128)
+        over_rows = (((0,), (0,)), ((), ()))
+        acc[0, o] = lax.dot_general(left_, gx[...].reshape(NB * rows, 512), over_rows, preferred_element_type=F32)
+        acc[1, o] = lax.dot_general(left_, gp[...].reshape(NB * rows, 512), over_rows, preferred_element_type=F32)
+        swap(o).start()
+
+    def wgrad_send(t):
+        o = nth(t)
+        swap(o).wait_recv()
+        acc[k, o] = acc[k, o] + pair[o]
         for d in (1, 3, 2):
-            scatter(d, c).start()
-
-        @pl.when(c > 0)
-        def _():
-            reduce_step(c - 1)
-
-        return 0
-
-    lax.fori_loop(0, NB // 2, back_step, 0)
-    reduce_step(NB // 2 - 1)
-
-    for r in range(2):
-        for k_ in range(2):
+            wgrad_to(d, o).start()
+
+        @pl.when(k == x // 2)
+        def _():
             pltpu.make_async_copy(
-                acc.at[0, :, pl.ds(0, 128)], wg.at[k_, pl.ds(r * 512, 512)], wo_r.at[r, k_]
-            ).wait()
-    wg_out = pltpu.make_async_copy(wg, wgrad_ref, out_s.at[0])
-    wg_out.start()
+                acc.at[k, o, :, lanes(x)], wg.at[k, owner_rows(o)], wo_r.at[x % 2, k, o]
+            ).start()
+
+        @pl.when(k != x // 2)
+        def _():
+            wgrad_to(0, o).start()
+
+    def wgrad_step(t, _):
+        @pl.when(t < 4)
+        def _():
+            wgrad_product(t)
+
+        @pl.when(t > 0)
+        def _():
+            wgrad_send(t - 1)
+
+        return 0
+
+    lax.fori_loop(0, 5, wgrad_step, 0)
 
     def returned(l, _):
         pltpu.make_async_copy(fin.at[0], ret.at[l], rt_r.at[l]).wait()
@@ -318,11 +376,22 @@
     back_out = pltpu.make_async_copy(ret, back_ref, out_s.at[1])
     back_out.start()
 
+    def owned(o, _):
+        for r in range(2):
+            for k_ in range(2):
+                at = pl.ds(pl.multiple_of(r * 512 + o * 128, 128), 128)
+                pltpu.make_async_copy(acc.at[0, 0, :, pl.ds(0, 128)], wg.at[k_, at], wo_r.at[r, k_, o]).wait()
+        return 0
+
+    lax.fori_loop(0, NZ, owned, 0)
+    wg_out = pltpu.make_async_copy(wg, wgrad_ref, out_s.at[0])
+    wg_out.start()
+
     def drain(b, _):
         drain_line(xz, b, xr_s, xl_s, xz_r)
         drain_line(gz, b, gr_s, gl_s, gz_r)
-        for d in (1, 2, 3):
-            ring(d, b).wait_send()
+        for send in (0, 1, 2):
+            remote(blk(gx, b, x), blk(gx, b, x), gx_s.at[send, b], gx_r.at[0, b], dev(zh, y, 1 - k, x, zl)).wait_send()
 
         @pl.when(jnp.logical_or(zh != k, b != zh * 4 + y))
         def _():
@@ -339,20 +408,27 @@
     lax.fori_loop(0, NB, drain, 0)
 
     def drain_scatter(c, _):
-        for d in (1, 2, 3):
-            scatter(d, c).wait_send()
+        for way in (0, 1):
+            far(way, c).wait_send()
+            near(way, c).wait_send()
         return 0
 
     lax.fori_loop(0, NB // 2, drain_scatter, 0)
     for copy in w_copies:
         copy.wait_send()
-    swap.wait_send()
-    for d in (1, 2, 3):
-        wgrad_to(d).wait_send()
-
-    @pl.when(k != x // 2)
-    def _():
-        wgrad_to(0).wait_send()
+
+    def drain_wgrad(o, _):
+        swap(o).wait_send()
+        for d in (1, 2, 3):
+            wgrad_to(d, o).wait_send()
+
+        @pl.when(k != x // 2)
+        def _():
+            wgrad_to(0, o).wait_send()
+
+        return 0
+
+    lax.fori_loop(0, NZ, drain_wgrad, 0)
 
     wg_out.wait()
     back_out.wait()
@@ -390,17 +466,19 @@
             vmem((NB, rows, 512), BF16),
             vmem((NB, rows, 512), BF16),
             vmem((NB, rows, 512), BF16),
+            vmem((NB, rows, 512), BF16),
             vmem((2, 4, 128, 512), BF16),
-            vmem((2, 512, 512), F32),
-            vmem((512, 512), F32),
+            vmem((2, NZ, 128, 512), F32),
+            vmem((NZ, 128, 512), F32),
             vmem((NX, NB, rows, 128), F32),
-            vmem((3, NB, rows, 128), F32),
+            vmem((2, NB, half, 128), F32),
+            vmem((2, NB, rows, 128), F32),
             vmem((NB, rows, 128), F32),
             vmem((NB, rows, 128), F32),
             vmem((2, 1024, 128), F32),
             dma((8,)), dma((8,)), dma((8,)), dma((8,)), dma((8,)), dma((8,)), dma((4,)), dma((4,)), dma(()),
-            dma((4, 8)), dma((4, 8)), dma((4, 8)), dma((4, 8)), dma((4, 8)), dma((4, 8)), dma((4, 8)), dma((4, 8)),
-            dma(()), dma(()), dma((4,)), dma((2, 2)), dma((3, 4)), dma((3, 4)), dma((8,)), dma((8,)), dma((2,)),
+            dma((4, 8)), dma((4, 8)), dma((4, 8)), dma((4, 8)), dma((4, 8)), dma((4, 8)), dma((3, 8)), dma((3, 8)),
+            dma((4,)), dma((4,)), dma((4, 4)), dma((2, 2, 4)), dma((2, 4)), dma((2, 4)), dma((2, 4)), dma((2, 4)), dma((8,)), dma((8,)), dma((2,)),
         ],
         compiler_params=pltpu.CompilerParams(
             collective_id=0, has_side_effects=True, vmem_limit_bytes=44 * 2**20

time: 153 us -> 118 us (0.77)
  Pallas kernels: 148 us -> 112 us
    pallas_call x1, Pallas kernels: 148 us -> 112 us  [per_device(): pl.pallas_call(functools.partial(kernel, rows), name='mix_back', out_shap...]
where the time goes in v2:
time: 118 us
  Pallas kernels  112 us (95%)
  local copies, waits for them, and re-layouts  2.56 us (2%)
  between operations  1.34 us (1%)
  other arithmetic  1.3 us (1%)
    pallas_call x1, Pallas kernels, per_device(): pl.pallas_call(functools.partial(kernel, rows), name='mix_back', out_shap...  112 us

profile of v2, /device:TPU:1, one launch (start us, length us, event | category | flops | bytes accessed | tf_op | source)
XLA Modules:
  0.0 117.7 jit_solution(4600157082557315539)
XLA Ops:
  1.3 0.1 compare_convert_fusion
  1.4 0.1 copy.9
  1.5 1.2 %broadcast_multiply_fusion = (bf16[2,2,8,45,128]{4,2,3,1,0:T(8,128)(2,1)S(1)}, bf16[2,2,8,45,128]{4,2,3,1,0:T(8,128)(2,1)S(1)}) fusion(bf16[2,2,8,45,128]{4,2,3,1,0:T(8,128)(2,1)} %param.6, bf16[8,45]{0,1:T(8,128)(2,1)S(1)} %copy.9, bf16[2,2,8,45,128]{4,2,3,1,0:T(8,128)(2,1)} %param.5), kind=kLoop, calls=%fused_computation | loop fusion | flops 368640 | bytes 1475280 | tf_op jit(solution)/shard_map/mul | solution.py:448
  2.7 0.1 copy.10
  2.8 0.1 copy.11
  2.9 112.5 %mix_back.1 = (f32[8,192,128]{2,1,0:T(8,128)S(1)}, f32[2,1024,128]{2,1,0:T(8,128)S(1)}) custom-call(bf16[8,192,128]{2,1,0:T(8,128)(2,1)S(1)} %bitcast.16, bf16[8,192,128]{2,1,0:T(8,128)(2,1)S(1)} %bitcast.17, bf16[2,8,4,4,128,128]{5,4,3,2,1,0:T(8,128)(2,1)} %bitcast.19), custom_call_target="tpu_custom_call" | custom-call | tf_op jit(solution)/shard_map/mix_back/pallas_call | solution.py:452
  115.4 1.3 %copy.12 = f32[8,2,90,128]{3,0,2,1:T(8,128)} copy(f32[8,2,90,128]{3,2,1,0:T(8,128)S(1)} %bitcast.18) | data formatting | bytes 1474560 | tf_op jit(solution)/shard_map/slice | solution.py:487
  116.7 1.0 copy.15
  (4 shorter events, 0.1 us)

commit v3 on v2

--- a/solution.py
+++ b/solution.py
@@ -25,8 +25,8 @@
 
 def kernel(
     rows, x_ref, g_ref, w_ref, back_ref, wgrad_ref,
-    xz, gx, gp, gz, wt, acc, pair, part, relay, heap, fin, ret, wg,
-    xa_s, xa_r, ga_s, ga_r, gi_s, gi_r, w_s, w_r, w_loc,
+    xz, xc, xt, gx, gp, gz, wt, acc, pair, part, relay, heap, fin, ret, wg,
+    xa_s, xa_r, xc_r, xc_s, xt_r, ga_s, ga_r, gi_s, gi_r, w_s, w_r, w_loc,
     xr_s, xl_s, xz_r, gr_s, gl_s, gz_r, gx_s, gx_r,
     pair_s, pair_r, wo_s, wo_r, far_s, far_r, rs_s, rs_r, rt_s, rt_r, out_s,
 ):
@@ -102,6 +102,28 @@
     degree = 4 * k + y
     pltpu.make_async_copy(g_ref.at[degree], blk(gz, me, zl), gi_r.at[me]).start()
     weight_out(g_ref, gx, x, ga_s, ga_r)
+
+    source = zh == k
+
+    def x_out(t, _):
+        y_ = (y + t) % 4
+        mine, other = zh * 4 + y_, (1 - zh) * 4 + y_
+        itself = jnp.logical_and(source, t == 0)
+
+        @pl.when(itself)
+        def _():
+            pltpu.make_async_copy(x_ref.at[mine], blk(xz, me, zl), xa_r.at[me]).start()
+            pltpu.make_async_copy(x_ref.at[other], xc.at[me], xc_r.at[me]).start()
+
+        @pl.when(jnp.logical_not(itself))
+        def _():
+            to = dev(zh, y_, zh, x, zl)
+            remote(x_ref.at[mine], blk(xz, me, zl), xa_s.at[mine], xa_r.at[me], to).start()
+            remote(x_ref.at[other], xc.at[me], xa_s.at[other], xc_r.at[me], to).start()
+
+        return 0
+
+    lax.fori_loop(0, 4, x_out, 0)
 
     w_loc_copy = pltpu.make_async_copy(w_ref.at[:, degree, :, zl], wt.at[:, :, :, lanes(zl)], w_loc)
     w_loc_copy.start()
@@ -180,14 +202,82 @@
         for b in pair_of(c):
             pass_line(gz, b, d, gr_s, gl_s, gz_r)
 
+    def x_right(src, o, b, send):
+        return remote(src, blk(xz, b, o), send, xz_r.at[o, b], at_z((z + 1) % 8))
+
+    def x_left(src, o, b, send):
+        return remote(src, blk(xz, b, o), send, xz_r.at[o, b], at_z((z + 7) % 8))
+
+    def transit(b, d):
+        return remote(xc.at[b], xt.at[b], xc_s.at[0, b], xt_r.at[b], at_z((z + d) % 8))
+
+    def x_cross(b):
+        @pl.when(zl == 3)
+        def _():
+            x_right(xc.at[b], 3, b, xc_s.at[0, b]).start()
+
+        @pl.when(zl == 0)
+        def _():
+            x_left(xc.at[b], 0, b, xc_s.at[0, b]).start()
+
+        @pl.when(zl == 2)
+        def _():
+            transit(b, 1).start()
+
+        @pl.when(zl == 1)
+        def _():
+            transit(b, 7).start()
+
+    def x_transit(b):
+        @pl.when(zl == 3)
+        def _():
+            transit(b, 1).wait_recv()
+            x_right(xt.at[b], 2, b, xc_s.at[1, b]).start()
+
+        @pl.when(zl == 0)
+        def _():
+            transit(b, 7).wait_recv()
+            x_left(xt.at[b], 1, b, xc_s.at[1, b]).start()
+
     def x_own(c):
-        for b in pair_of(c):
-            pltpu.make_async_copy(x_ref.at[0], blk(xz, b, zl), xa_r.at[b]).wait()
-            own_line(xz, b, xr_s, xl_s, xz_r)
-
-    def x_pass(c, d):
-        for b in pair_of(c):
-            pass_line(xz, b, d, xr_s, xl_s, xz_r)
+        @pl.when(source)
+        def _():
+            for b in pair_of(c):
+                pltpu.make_async_copy(x_ref.at[0], xc.at[b], xc_r.at[b]).wait()
+                x_cross(b)
+                pltpu.make_async_copy(x_ref.at[0], blk(xz, b, zl), xa_r.at[b]).wait()
+                own_line(xz, b, xr_s, xl_s, xz_r)
+
+    def x_arrive(b, o, to_right):
+        if to_right:
+            x_right(blk(xz, b, o), o, b, xr_s.at[o, b]).wait_recv()
+
+            @pl.when(zl < 3)
+            def _():
+                x_right(blk(xz, b, o), o, b, xr_s.at[o, b]).start()
+        else:
+            x_left(blk(xz, b, o), o, b, xl_s.at[o, b]).wait_recv()
+
+            @pl.when(zl > 0)
+            def _():
+                x_left(blk(xz, b, o), o, b, xl_s.at[o, b]).start()
+
+    def x_hop(c, hops):
+        @pl.when(source)
+        def _():
+            for b in pair_of(c):
+                if hops == 1:
+                    x_transit(b)
+                if hops <= 3:
+                    pass_line(xz, b, hops, xr_s, xl_s, xz_r)
+
+        @pl.when(jnp.logical_not(source))
+        def _():
+            for b in pair_of(c):
+                for o, first in ((3, zl + 1), (2, zl + 2), (0, 4 - zl), (1, 5 - zl)):
+                    @pl.when(first == hops)
+                    def _():
+                        x_arrive(b, o, o >= 2)
 
     def ring_own(c):
         for b in pair_of(c):
@@ -270,44 +360,9 @@
         for way in (0, 1):
             far(way, c).start()
 
-    def when_chunk(c, work):
-        @pl.when((c >= 0) & (c < 4))
-        def _():
-            work(c)
-
-    def pipeline(s, _):
-        when_chunk(s, g_own)
-        when_chunk(s - 1, lambda c: g_pass(c, 1))
-        when_chunk(s - 1, ring_own)
-        when_chunk(s - 2, lambda c: g_pass(c, 2))
-
-        @pl.when(s == 3)
-        def _():
-            weight_out(x_ref, xz, zl, xa_s, xa_r)
-            w_loc_copy.wait()
-            for copy in w_copies:
-                copy.wait_recv()
-
-        def product(c):
-            g_pass(c, 3)
-            back_product(c)
-
-        when_chunk(s - 3, product)
-        when_chunk(s - 2, ring_pass)
-        when_chunk(s - 4, back_relay)
-        when_chunk(s - 5, x_own)
-        when_chunk(s - 5, back_reduce)
-        when_chunk(s - 6, lambda c: x_pass(c, 1))
-        when_chunk(s - 6, ring_end)
-        when_chunk(s - 7, lambda c: x_pass(c, 2))
-        return 0
-
-    lax.fori_loop(0, 11, pipeline, 0)
-
-    order_of = jnp.where(zl == 0, 0o3210, jnp.where(zl == 1, 0o3201, jnp.where(zl == 2, 0o0312, 0o0123)))
-
     def nth(t):
-        return (order_of // jnp.where(t == 0, 1, jnp.where(t == 1, 8, jnp.where(t == 2, 64, 512)))) % 8
+        o = 3 - t if t < 2 else t - 2
+        return jnp.where(zl < 2, o, 3 - o)
 
     def swap(o):
         return remote(acc.at[1 - k, o], pair.at[o], pair_s.at[o], pair_r.at[o], dev(zh, y, 1 - k, x, zl))
@@ -323,14 +378,6 @@
 
     def wgrad_product(t):
         o = nth(t)
-
-        @pl.when(t == 3)
-        def _():
-            def last(b, _):
-                pass_line(xz, b, 3, xr_s, xl_s, xz_r)
-                return 0
-
-            lax.fori_loop(0, NB, last, 0)
 
         left_ = xz[:, :, lanes(o)].reshape(NB * rows, 128)
         over_rows = (((0,), (0,)), ((), ()))
@@ -355,18 +402,56 @@
         def _():
             wgrad_to(0, o).start()
 
-    def wgrad_step(t, _):
-        @pl.when(t < 4)
-        def _():
-            wgrad_product(t)
-
-        @pl.when(t > 0)
-        def _():
-            wgrad_send(t - 1)
-
-        return 0
-
-    lax.fori_loop(0, 5, wgrad_step, 0)
+    def when_chunk(c, work):
+        @pl.when((c >= 0) & (c < 4))
+        def _():
+            work(c)
+
+    def pipeline(s, _):
+        when_chunk(s, g_own)
+        when_chunk(s - 1, lambda c: g_pass(c, 1))
+        when_chunk(s - 1, ring_own)
+        when_chunk(s - 2, lambda c: g_pass(c, 2))
+
+        @pl.when(s == 3)
+        def _():
+            w_loc_copy.wait()
+            for copy in w_copies:
+                copy.wait_recv()
+
+        def product(c):
+            g_pass(c, 3)
+            back_product(c)
+
+        when_chunk(s - 3, product)
+        when_chunk(s - 2, ring_pass)
+        when_chunk(s - 3, x_own)
+        when_chunk(s - 4, back_relay)
+        when_chunk(s - 4, lambda c: x_hop(c, 1))
+        when_chunk(s - 5, back_reduce)
+        when_chunk(s - 5, lambda c: x_hop(c, 2))
+        when_chunk(s - 5, ring_end)
+        when_chunk(s - 6, lambda c: x_hop(c, 3))
+        when_chunk(s - 7, lambda c: x_hop(c, 4))
+
+        @pl.when(s == 10)
+        def _():
+            wgrad_product(0)
+            wgrad_product(1)
+
+        @pl.when(s == 11)
+        def _():
+            wgrad_send(0)
+            wgrad_product(2)
+            wgrad_send(1)
+
+        when_chunk(s - 8, lambda c: x_hop(c, 5))
+        return 0
+
+    lax.fori_loop(0, 12, pipeline, 0)
+    wgrad_product(3)
+    wgrad_send(2)
+    wgrad_send(3)
 
     def returned(l, _):
         pltpu.make_async_copy(fin.at[0], ret.at[l], rt_r.at[l]).wait()
@@ -388,15 +473,38 @@
     wg_out.start()
 
     def drain(b, _):
-        drain_line(xz, b, xr_s, xl_s, xz_r)
+        @pl.when(source)
+        def _():
+            drain_line(xz, b, xr_s, xl_s, xz_r)
+            x_right(xc.at[b], 3, b, xc_s.at[0, b]).wait_send()
+
+            @pl.when((zl == 0) | (zl == 3))
+            def _():
+                x_right(xt.at[b], 2, b, xc_s.at[1, b]).wait_send()
+
+        @pl.when(jnp.logical_not(source))
+        def _():
+            for o in (0, 1, 2, 3):
+                if o >= 2:
+                    @pl.when(zl < 3)
+                    def _():
+                        x_right(blk(xz, b, o), o, b, xr_s.at[o, b]).wait_send()
+                else:
+                    @pl.when(zl > 0)
+                    def _():
+                        x_left(blk(xz, b, o), o, b, xl_s.at[o, b]).wait_send()
+
         drain_line(gz, b, gr_s, gl_s, gz_r)
         for send in (0, 1, 2):
             remote(blk(gx, b, x), blk(gx, b, x), gx_s.at[send, b], gx_r.at[0, b], dev(zh, y, 1 - k, x, zl)).wait_send()
 
         @pl.when(jnp.logical_or(zh != k, b != zh * 4 + y))
         def _():
+            pltpu.make_async_copy(g_ref.at[b], blk(gx, 0, x), ga_s.at[b]).wait()
+
+        @pl.when(jnp.logical_or(zh != k, b % 4 != y))
+        def _():
             pltpu.make_async_copy(x_ref.at[b], blk(xz, 0, zl), xa_s.at[b]).wait()
-            pltpu.make_async_copy(g_ref.at[b], blk(gx, 0, x), ga_s.at[b]).wait()
 
         @pl.when(b != me)
         def _():
@@ -464,6 +572,8 @@
         out_specs=(pl.BlockSpec(memory_space=pl.ANY), pl.BlockSpec(memory_space=pl.ANY)),
         scratch_shapes=[
             vmem((NB, rows, 512), BF16),
+            vmem((NB, rows, 128), BF16),
+            vmem((NB, rows, 128), BF16),
             vmem((NB, rows, 512), BF16),
             vmem((NB, rows, 512), BF16),
             vmem((NB, rows, 512), BF16),
@@ -476,7 +586,8 @@
             vmem((NB, rows, 128), F32),
             vmem((NB, rows, 128), F32),
             vmem((2, 1024, 128), F32),
-            dma((8,)), dma((8,)), dma((8,)), dma((8,)), dma((8,)), dma((8,)), dma((4,)), dma((4,)), dma(()),
+            dma((8,)), dma((8,)), dma((8,)), dma((2, 8)), dma((8,)),
+            dma((8,)), dma((8,)), dma((8,)), dma((8,)), dma((4,)), dma((4,)), dma(()),
             dma((4, 8)), dma((4, 8)), dma((4, 8)), dma((4, 8)), dma((4, 8)), dma((4, 8)), dma((3, 8)), dma((3, 8)),
             dma((4,)), dma((4,)), dma((4, 4)), dma((2, 2, 4)), dma((2, 4)), dma((2, 4)), dma((2, 4)), dma((2, 4)), dma((8,)), dma((8,)), dma((2,)),
         ],

time: 118 us -> 109 us (0.924)
  Pallas kernels: 112 us -> 104 us
    pallas_call x1, Pallas kernels: 112 us -> 104 us  [per_device(): pl.pallas_call(functools.partial(kernel, rows), name='mix_back', out_shap...]
where the time goes in v3:
time: 109 us
  Pallas kernels  104 us (95%)
  local copies, waits for them, and re-layouts  2.56 us (2%)
  between operations  1.34 us (1%)
  other arithmetic  1.3 us (1%)
    pallas_call x1, Pallas kernels, per_device(): pl.pallas_call(functools.partial(kernel, rows), name='mix_back', out_shap...  104 us

profile of v3, /device:TPU:1, one launch (start us, length us, event | category | flops | bytes accessed | tf_op | source)
XLA Modules:
  0.0 109.0 jit_solution(5219382260728988632)
XLA Ops:
  1.3 0.1 compare_convert_fusion
  1.4 0.1 copy.9
  1.5 1.2 %broadcast_multiply_fusion = (bf16[2,2,8,45,128]{4,2,3,1,0:T(8,128)(2,1)S(1)}, bf16[2,2,8,45,128]{4,2,3,1,0:T(8,128)(2,1)S(1)}) fusion(bf16[2,2,8,45,128]{4,2,3,1,0:T(8,128)(2,1)} %param.6, bf16[8,45]{0,1:T(8,128)(2,1)S(1)} %copy.9, bf16[2,2,8,45,128]{4,2,3,1,0:T(8,128)(2,1)} %param.5), kind=kLoop, calls=%fused_computation | loop fusion | flops 368640 | bytes 1475280 | tf_op jit(solution)/shard_map/mul | solution.py:556
  2.7 0.1 copy.10
  2.8 0.1 copy.11
  2.9 103.8 %mix_back.1 = (f32[8,192,128]{2,1,0:T(8,128)S(1)}, f32[2,1024,128]{2,1,0:T(8,128)S(1)}) custom-call(bf16[8,192,128]{2,1,0:T(8,128)(2,1)S(1)} %bitcast.16, bf16[8,192,128]{2,1,0:T(8,128)(2,1)S(1)} %bitcast.17, bf16[2,8,4,4,128,128]{5,4,3,2,1,0:T(8,128)(2,1)} %bitcast.19), custom_call_target="tpu_custom_call" | custom-call | tf_op jit(solution)/shard_map/mix_back/pallas_call | solution.py:560
  106.7 1.3 %copy.12 = f32[8,2,90,128]{3,0,2,1:T(8,128)} copy(f32[8,2,90,128]{3,2,1,0:T(8,128)S(1)} %bitcast.18) | data formatting | bytes 1474560 | tf_op jit(solution)/shard_map/slice | solution.py:598
  108.0 1.0 copy.15
  (4 shorter events, 0.1 us)

commit v4 on v3

--- a/solution.py
+++ b/solution.py
@@ -24,11 +24,11 @@
 
 
 def kernel(
-    rows, x_ref, g_ref, w_ref, back_ref, wgrad_ref,
-    xz, xc, xt, gx, gp, gz, wt, acc, pair, part, relay, heap, fin, ret, wg,
+    orders, rows, window_ref, x_hbm, g_hbm, w_ref, back_ref, wgrad_ref,
+    x_in, g_in, x_ref, g_ref, xz, xc, xt, gx, gp, gz, wt, acc, pair, part, relay, heap, fin, ret, wg,
     xa_s, xa_r, xc_r, xc_s, xt_r, ga_s, ga_r, gi_s, gi_r, w_s, w_r, w_loc,
     xr_s, xl_s, xz_r, gr_s, gl_s, gz_r, gx_s, gx_r,
-    pair_s, pair_r, wo_s, wo_r, far_s, far_r, rs_s, rs_r, rt_s, rt_r, out_s,
+    pair_s, pair_r, wo_s, wo_r, far_s, far_r, rs_s, rs_r, rt_s, rt_r, in_s, out_s,
 ):
     zh, y, k, x, zl = coords()
     z = zh * 4 + zl
@@ -44,18 +44,49 @@
     def greet(device):
         pl.semaphore_signal(pltpu.get_barrier_semaphore(), inc=1, device_id=device, device_id_type=MESH)
 
-    def greet_order(t, _):
-        other = (zh * 8 + me + t) % 16
-        greet((other, x * 4 + zl))
-        return 0
-
-    lax.fori_loop(1, 16, greet_order, 0)
-    for d in (1, 2, 3, 5, 6, 7):
+    x_load = pltpu.make_async_copy(x_hbm, x_in, in_s.at[0])
+    g_load = pltpu.make_async_copy(g_hbm, g_in, in_s.at[1])
+    g_load.start()
+    x_load.start()
+
+    def greet_half(t, _):
+        greet((zh * 8 + (me + t) % 8, x * 4 + zl))
+        return 0
+
+    lax.fori_loop(1, 8, greet_half, 0)
+
+    @pl.when(zh != k)
+    def _():
+        def greet_other(t, _):
+            greet(((1 - zh) * 8 + (me + t) % 8, x * 4 + zl))
+            return 0
+
+        lax.fori_loop(0, 8, greet_other, 0)
+
+    for d in (1, 2, 6, 7):
         greet(at_z((z + d) % 8))
     for d in (1, 2, 3):
         for other in (0, 1):
             greet(dev(zh, y, other, (x + d) % 4, zl))
-    pl.semaphore_wait(pltpu.get_barrier_semaphore(), 15 + 6 + 6)
+
+    def by_degree(raw, out):
+        step = half // raw.shape[1]
+        shape = (raw.shape[3], raw.shape[2], 128)
+        degree_of = window_ref[0] + lax.broadcasted_iota(jnp.int32, shape, 0)
+        order_of = (zh * 8 + me) * orders + lax.broadcasted_iota(jnp.int32, shape, 1)
+        live = jnp.where(order_of <= degree_of, 1.0, 0.0)
+        pad = jnp.zeros((shape[0], step - shape[1], 128), F32)
+        for part_ in range(raw.shape[0]):
+            for sample in range(raw.shape[1]):
+                values = jnp.swapaxes(raw[part_, sample].astype(F32), 0, 1) * live
+                at = pl.ds(part_ * half + sample * step, step)
+                out[:, at] = jnp.concatenate([values, pad], axis=1).astype(BF16)
+
+    g_load.wait()
+    by_degree(g_in, g_ref)
+    x_load.wait()
+    by_degree(x_in, x_ref)
+    pl.semaphore_wait(pltpu.get_barrier_semaphore(), 7 + 4 + 4 + 6)
 
     def remote(src, dst, send, recv, device):
         return pltpu.make_async_remote_copy(
@@ -101,8 +132,6 @@
     lax.fori_loop(1, 8, gi_step, 0)
     degree = 4 * k + y
     pltpu.make_async_copy(g_ref.at[degree], blk(gz, me, zl), gi_r.at[me]).start()
-    weight_out(g_ref, gx, x, ga_s, ga_r)
-
     source = zh == k
 
     def x_out(t, _):
@@ -124,6 +153,8 @@
         return 0
 
     lax.fori_loop(0, 4, x_out, 0)
+
+    weight_out(g_ref, gx, x, ga_s, ga_r)
 
     w_loc_copy = pltpu.make_async_copy(w_ref.at[:, degree, :, zl], wt.at[:, :, :, lanes(zl)], w_loc)
     w_loc_copy.start()
@@ -243,8 +274,6 @@
         @pl.when(source)
         def _():
             for b in pair_of(c):
-                pltpu.make_async_copy(x_ref.at[0], xc.at[b], xc_r.at[b]).wait()
-                x_cross(b)
                 pltpu.make_async_copy(x_ref.at[0], blk(xz, b, zl), xa_r.at[b]).wait()
                 own_line(xz, b, xr_s, xl_s, xz_r)
 
@@ -262,14 +291,19 @@
             def _():
                 x_left(blk(xz, b, o), o, b, xl_s.at[o, b]).start()
 
-    def x_hop(c, hops):
+    def x_start(c):
         @pl.when(source)
         def _():
             for b in pair_of(c):
-                if hops == 1:
+                pltpu.make_async_copy(x_ref.at[0], xc.at[b], xc_r.at[b]).wait()
+                x_cross(b)
+
+    def x_round(c, hops):
+        if hops == 1:
+            @pl.when(source)
+            def _():
+                for b in pair_of(c):
                     x_transit(b)
-                if hops <= 3:
-                    pass_line(xz, b, hops, xr_s, xl_s, xz_r)
 
         @pl.when(jnp.logical_not(source))
         def _():
@@ -278,6 +312,12 @@
                     @pl.when(first == hops)
                     def _():
                         x_arrive(b, o, o >= 2)
+
+    def x_pass(c, d):
+        @pl.when(source)
+        def _():
+            for b in pair_of(c):
+                pass_line(xz, b, d, xr_s, xl_s, xz_r)
 
     def ring_own(c):
         for b in pair_of(c):
@@ -361,8 +401,11 @@
             far(way, c).start()
 
     def nth(t):
-        o = 3 - t if t < 2 else t - 2
-        return jnp.where(zl < 2, o, 3 - o)
+        if t == 0:
+            return zl
+        if t == 1:
+            return zl + 1 - 2 * (zl % 2)
+        return jnp.where(zl < 2, t, 3 - t)
 
     def swap(o):
         return remote(acc.at[1 - k, o], pair.at[o], pair_s.at[o], pair_r.at[o], dev(zh, y, 1 - k, x, zl))
@@ -409,9 +452,12 @@
 
     def pipeline(s, _):
         when_chunk(s, g_own)
+        when_chunk(s, x_start)
         when_chunk(s - 1, lambda c: g_pass(c, 1))
+        when_chunk(s - 1, lambda c: x_round(c, 1))
         when_chunk(s - 1, ring_own)
         when_chunk(s - 2, lambda c: g_pass(c, 2))
+        when_chunk(s - 2, lambda c: x_round(c, 2))
 
         @pl.when(s == 3)
         def _():
@@ -424,31 +470,38 @@
             back_product(c)
 
         when_chunk(s - 3, product)
+        when_chunk(s - 3, x_own)
+        when_chunk(s - 3, lambda c: x_round(c, 3))
         when_chunk(s - 2, ring_pass)
-        when_chunk(s - 3, x_own)
         when_chunk(s - 4, back_relay)
-        when_chunk(s - 4, lambda c: x_hop(c, 1))
+        when_chunk(s - 4, lambda c: x_round(c, 4))
+        when_chunk(s - 3, ring_end)
+        when_chunk(s - 5, lambda c: x_round(c, 5))
         when_chunk(s - 5, back_reduce)
-        when_chunk(s - 5, lambda c: x_hop(c, 2))
-        when_chunk(s - 5, ring_end)
-        when_chunk(s - 6, lambda c: x_hop(c, 3))
-        when_chunk(s - 7, lambda c: x_hop(c, 4))
-
-        @pl.when(s == 10)
-        def _():
-            wgrad_product(0)
-            wgrad_product(1)
-
-        @pl.when(s == 11)
-        def _():
-            wgrad_send(0)
-            wgrad_product(2)
-            wgrad_send(1)
-
-        when_chunk(s - 8, lambda c: x_hop(c, 5))
-        return 0
-
-    lax.fori_loop(0, 12, pipeline, 0)
+        return 0
+
+    def every(work):
+        def step(c, _):
+            work(c)
+            return 0
+
+        lax.fori_loop(0, 4, step, 0)
+
+    lax.fori_loop(0, 7, pipeline, 0)
+    x_round(3, 4)
+    x_round(2, 5)
+    x_round(3, 5)
+    every(lambda c: x_pass(c, 1))
+    back_relay(3)
+    wgrad_product(0)
+    back_reduce(2)
+    wgrad_product(1)
+    wgrad_send(0)
+    every(lambda c: x_pass(c, 2))
+    wgrad_product(2)
+    wgrad_send(1)
+    back_reduce(3)
+    every(lambda c: x_pass(c, 3))
     wgrad_product(3)
     wgrad_send(2)
     wgrad_send(3)
@@ -544,33 +597,30 @@
 
 def per_device(window, inputs, out_grad, weights):
     _, samples, degrees, orders, width = inputs.shape
-    first_order = lax.axis_index("order") * orders
-    degree = window[0] + jnp.arange(degrees, dtype=jnp.int32)
-    order = first_order + jnp.arange(orders, dtype=jnp.int32)
-    live = (order[None, :] <= degree[:, None]).astype(BF16)[:, :, None]
-    real = samples * orders
-    half = -(-real // 16) * 16
+    step = -(-orders // 16) * 16
+    half = samples * step
     rows = 2 * half
-
-    def by_degree(a):
-        a = (a * live).transpose(2, 0, 1, 3, 4).reshape(degrees, 2, real, width)
-        return jnp.pad(a, ((0, 0), (0, 0), (0, half - real), (0, 0))).reshape(degrees, rows, width)
 
     dma, vmem = pltpu.SemaphoreType.DMA, pltpu.VMEM
     back, wgrad = pl.pallas_call(
-        functools.partial(kernel, rows),
+        functools.partial(kernel, orders, rows),
         name="mix_back",
         out_shape=(
             jax.ShapeDtypeStruct((degrees, rows, width), F32),
             jax.ShapeDtypeStruct((2, 1024, width), F32),
         ),
         in_specs=[
-            pl.BlockSpec(memory_space=pltpu.VMEM),
-            pl.BlockSpec(memory_space=pltpu.VMEM),
+            pl.BlockSpec(memory_space=pltpu.SMEM),
+            pl.BlockSpec(memory_space=pl.ANY),
+            pl.BlockSpec(memory_space=pl.ANY),
             pl.BlockSpec(memory_space=pl.ANY),
         ],
         out_specs=(pl.BlockSpec(memory_space=pl.ANY), pl.BlockSpec(memory_space=pl.ANY)),
         scratch_shapes=[
+            vmem((2, samples, orders, degrees, width), BF16),
+            vmem((2, samples, orders, degrees, width), BF16),
+            vmem((degrees, rows, width), BF16),
+            vmem((degrees, rows, width), BF16),
             vmem((NB, rows, 512), BF16),
             vmem((NB, rows, 128), BF16),
             vmem((NB, rows, 128), BF16),
@@ -589,13 +639,18 @@
             dma((8,)), dma((8,)), dma((8,)), dma((2, 8)), dma((8,)),
             dma((8,)), dma((8,)), dma((8,)), dma((8,)), dma((4,)), dma((4,)), dma(()),
             dma((4, 8)), dma((4, 8)), dma((4, 8)), dma((4, 8)), dma((4, 8)), dma((4, 8)), dma((3, 8)), dma((3, 8)),
-            dma((4,)), dma((4,)), dma((4, 4)), dma((2, 2, 4)), dma((2, 4)), dma((2, 4)), dma((2, 4)), dma((2, 4)), dma((8,)), dma((8,)), dma((2,)),
+            dma((4,)), dma((4,)), dma((4, 4)), dma((2, 2, 4)), dma((2, 4)), dma((2, 4)), dma((2, 4)), dma((2, 4)), dma((8,)), dma((8,)), dma((2,)), dma((2,)),
         ],
         compiler_params=pltpu.CompilerParams(
             collective_id=0, has_side_effects=True, vmem_limit_bytes=44 * 2**20
         ),
-    )(by_degree(inputs), by_degree(out_grad), weights.reshape(2, degrees, 4, 4, 128, width))
-    back = back.reshape(degrees, 2, half, width)[:, :, :real].reshape(degrees, 2, samples, orders, width)
+    )(
+        window,
+        inputs.transpose(0, 1, 3, 2, 4),
+        out_grad.transpose(0, 1, 3, 2, 4),
+        weights.reshape(2, degrees, 4, 4, 128, width),
+    )
+    back = back.reshape(degrees, 2, samples, step, width)[:, :, :, :orders]
     return back.transpose(1, 2, 0, 3, 4), wgrad
 
 

time: 109 us -> 106 us (0.972)
  Pallas kernels: 104 us -> 99.9 us
  local copies, waits for them, and re-layouts: 2.56 us -> 4.23 us
  other arithmetic: 1.3 us -> 0 us
    pallas_call x1, Pallas kernels: 104 us -> 99.9 us  [per_device(): pl.pallas_call(functools.partial(kernel, orders, rows), name='mix_back',...]
    unnamed x1 -> x6, local copies, waits for them, and re-layouts: 0.97 us -> 4.23 us
    slice x1 -> x0, local copies, waits for them, and re-layouts: 1.29 us -> none  [per_device(): back.reshape(degrees, 2, half, width)[:, :, :real]]
    mul x1 -> x0, other arithmetic: 1.22 us -> none  [by_degree(): a = (a * live).transpose(2, 0, 1, 3, 4).reshape(degrees, 2, real, width)]
where the time goes in v4:
time: 106 us; the launch traced here: 105 us
  Pallas kernels  99.9 us (94%)
  local copies, waits for them, and re-layouts  4.23 us (4%)
  between operations  1.29 us (1%)
    pallas_call x1, Pallas kernels, per_device(): pl.pallas_call(functools.partial(kernel, orders, rows), name='mix_back',...  99.9 us
    unnamed x6, local copies, waits for them, and re-layouts  4.23 us

profile of v4, /device:TPU:1, one launch (start us, length us, event | category | flops | bytes accessed | tf_op | source)
XLA Modules:
  0.0 105.4 jit_solution(2410665696225631109)
XLA Ops:
  1.3 0.0 copy-start
  1.3 1.0 copy-done
  2.3 0.0 copy-start.1
  2.3 1.0 copy-done.1
  3.3 99.9 %mix_back.1 = (f32[8,192,128]{2,1,0:T(8,128)S(1)}, f32[2,1024,128]{2,1,0:T(8,128)S(1)}) custom-call(s32[1]{0:T(128)S(6)} %copy.11.window_ref, bf16[2,2,45,8,128]{4,3,2,1,0:T(8,128)(2,1)S(1)} %bitcast.9, bf16[2,2,45,8,128]{4,3,2,1,0:T(8,128)(2,1)S(1)} %bitcast.10, bf16[2,8,4,4,128,128]{5,4,3,2,1,0:T(8,128)(2,1)} %bitcast.11), custom_call_target="tpu_custom_call" | custom-call | tf_op jit(solution)/shard_map/mix_back/pallas_call | solution.py:605
  103.1 1.3 %copy.9 = f32[8,2,2,45,128]{4,0,3,2,1:T(8,128)} copy(f32[8,2,2,45,128]{4,3,2,1,0:T(8,128)S(1)} %bitcast.8) | data formatting | bytes 1474560
  104.4 1.0 copy.12
Async XLA Ops:
  1.3 1.0 copy-start
  2.3 1.0 copy-start.1

commit v5 on v4

--- a/solution.py
+++ b/solution.py
@@ -25,10 +25,10 @@
 
 def kernel(
     orders, rows, window_ref, x_hbm, g_hbm, w_ref, back_ref, wgrad_ref,
-    x_in, g_in, x_ref, g_ref, xz, xc, xt, gx, gp, gz, wt, acc, pair, part, relay, heap, fin, ret, wg,
-    xa_s, xa_r, xc_r, xc_s, xt_r, ga_s, ga_r, gi_s, gi_r, w_s, w_r, w_loc,
+    x_in, g_in, x_ref, g_ref, xz, xc, xt, gx, gp, gz, wt, acc, pair, part, relay, heap, fin,
+    xa_s, xa_r, xc_r, xc_s, xt_r, gc_s, gc_r, gi_s, gi_r, w_s, w_r, w_loc,
     xr_s, xl_s, xz_r, gr_s, gl_s, gz_r, gx_s, gx_r,
-    pair_s, pair_r, wo_s, wo_r, far_s, far_r, rs_s, rs_r, rt_s, rt_r, in_s, out_s,
+    pair_s, pair_r, wo_s, wo_r, far_s, far_r, rs_s, rs_r, rt_s, rt_r, in_s,
 ):
     zh, y, k, x, zl = coords()
     z = zh * 4 + zl
@@ -57,11 +57,9 @@
 
     @pl.when(zh != k)
     def _():
-        def greet_other(t, _):
-            greet(((1 - zh) * 8 + (me + t) % 8, x * 4 + zl))
-            return 0
-
-        lax.fori_loop(0, 8, greet_other, 0)
+        end = jnp.where(zl < 2, 7 - zl, 4 - zl)
+        z_ = (z + end) % 8
+        greet(dev(z_ // 4, y, 1 - k, x, z_ % 4))
 
     for d in (1, 2, 6, 7):
         greet(at_z((z + d) % 8))
@@ -86,7 +84,16 @@
     by_degree(g_in, g_ref)
     x_load.wait()
     by_degree(x_in, x_ref)
-    pl.semaphore_wait(pltpu.get_barrier_semaphore(), 7 + 4 + 4 + 6)
+    at_end = jnp.logical_and(zh != k, jnp.logical_or(zl == 0, zl == 3))
+
+    @pl.when(at_end)
+    def _():
+        pl.semaphore_wait(pltpu.get_barrier_semaphore(), 7 + 4 + 6 + 2)
+
+    @pl.when(jnp.logical_not(at_end))
+    def _():
+        pl.semaphore_wait(pltpu.get_barrier_semaphore(), 7 + 4 + 6)
+
 
     def remote(src, dst, send, recv, device):
         return pltpu.make_async_remote_copy(
@@ -96,29 +103,8 @@
     def blk(buf, b, lane):
         return buf.at[b, :, lanes(lane)]
 
-    def to_weight(src, buf, lane, send, recv, t):
-        e = (zh * 4 + y + t) % 8
-        remote(src.at[e], blk(buf, me, lane), send.at[e], recv.at[me], dev(e // 4, e % 4, zh, x, zl)).start()
-
-    def own_weight(src, buf, lane, recv, e):
-        pltpu.make_async_copy(src.at[e], blk(buf, me, lane), recv.at[me]).start()
-
-    def weight_out(src, buf, lane, send, recv):
-        mine = zh == k
-
-        @pl.when(mine)
-        def _():
-            own_weight(src, buf, lane, recv, zh * 4 + y)
-
-        @pl.when(jnp.logical_not(mine))
-        def _():
-            to_weight(src, buf, lane, send, recv, 0)
-
-        def step(t, _):
-            to_weight(src, buf, lane, send, recv, t)
-            return 0
-
-        lax.fori_loop(1, 8, step, 0)
+    def two(buf, c, lane):
+        return buf.at[pl.ds(2 * c, 2), :, lanes(lane)]
 
     def to_input(t):
         j = (me + t) % 8
@@ -154,7 +140,6 @@
 
     lax.fori_loop(0, 4, x_out, 0)
 
-    weight_out(g_ref, gx, x, ga_s, ga_r)
 
     w_loc_copy = pltpu.make_async_copy(w_ref.at[:, degree, :, zl], wt.at[:, :, :, lanes(zl)], w_loc)
     w_loc_copy.start()
@@ -167,55 +152,55 @@
         )
         w_copies[-1].start()
 
-    def right(buf, o, b, send, recv):
-        return remote(blk(buf, b, o), blk(buf, b, o), send.at[o, b], recv.at[o, b], dev(zh, y, k, x, (zl + 1) % 4))
-
-    def left(buf, o, b, send, recv):
-        return remote(blk(buf, b, o), blk(buf, b, o), send.at[o, b], recv.at[o, b], dev(zh, y, k, x, (zl + 3) % 4))
-
-    def own_line(buf, b, s_r, s_l, recv):
+    def right(buf, o, c, send, recv):
+        return remote(two(buf, c, o), two(buf, c, o), send.at[o, c], recv.at[o, c], dev(zh, y, k, x, (zl + 1) % 4))
+
+    def left(buf, o, c, send, recv):
+        return remote(two(buf, c, o), two(buf, c, o), send.at[o, c], recv.at[o, c], dev(zh, y, k, x, (zl + 3) % 4))
+
+    def own_line(buf, c, s_r, s_l, recv):
         @pl.when(zl < 3)
         def _():
-            right(buf, zl, b, s_r, recv).start()
+            right(buf, zl, c, s_r, recv).start()
 
         @pl.when(zl > 0)
         def _():
-            left(buf, zl, b, s_l, recv).start()
-
-    def pass_line(buf, b, d, s_r, s_l, recv):
+            left(buf, zl, c, s_l, recv).start()
+
+    def pass_line(buf, c, d, s_r, s_l, recv):
         @pl.when(zl >= d)
         def _():
             o = zl - d
-            right(buf, o, b, s_r, recv).wait_recv()
+            right(buf, o, c, s_r, recv).wait_recv()
 
             @pl.when(zl < 3)
             def _():
-                right(buf, o, b, s_r, recv).start()
+                right(buf, o, c, s_r, recv).start()
 
         @pl.when(zl + d <= 3)
         def _():
             o = zl + d
-            left(buf, o, b, s_l, recv).wait_recv()
+            left(buf, o, c, s_l, recv).wait_recv()
 
             @pl.when(zl > 0)
             def _():
-                left(buf, o, b, s_l, recv).start()
-
-    def drain_line(buf, b, s_r, s_l, recv):
+                left(buf, o, c, s_l, recv).start()
+
+    def drain_line(buf, c, s_r, s_l, recv):
         for d in range(3):
             @pl.when((zl >= d) & (zl < 3))
             def _():
-                right(buf, zl - d, b, s_r, recv).wait_send()
+                right(buf, zl - d, c, s_r, recv).wait_send()
 
             @pl.when((zl + d <= 3) & (zl > 0))
             def _():
-                left(buf, zl + d, b, s_l, recv).wait_send()
-
-    def ring_right(o, b):
-        return remote(blk(gx, b, o), blk(gx, b, o), gx_s.at[0, b], gx_r.at[0, b], dev(zh, y, k, (x + 1) % 4, zl))
-
-    def ring_left(o, b):
-        return remote(blk(gx, b, o), blk(gx, b, o), gx_s.at[1, b], gx_r.at[1, b], dev(zh, y, k, (x + 3) % 4, zl))
+                left(buf, zl + d, c, s_l, recv).wait_send()
+
+    def ring_right(o, c):
+        return remote(two(gx, c, o), two(gx, c, o), gx_s.at[0, c], gx_r.at[0, c], dev(zh, y, k, (x + 1) % 4, zl))
+
+    def ring_left(o, c):
+        return remote(two(gx, c, o), two(gx, c, o), gx_s.at[1, c], gx_r.at[1, c], dev(zh, y, k, (x + 3) % 4, zl))
 
     def ring_far(to_right, b):
         o, to = ((x + 3) % 4, (x + 1) % 4) if to_right else ((x + 1) % 4, (x + 3) % 4)
@@ -227,109 +212,117 @@
     def g_own(c):
         for b in pair_of(c):
             pltpu.make_async_copy(g_ref.at[0], blk(gz, b, zl), gi_r.at[b]).wait()
-            own_line(gz, b, gr_s, gl_s, gz_r)
+        own_line(gz, c, gr_s, gl_s, gz_r)
+
+        @pl.when(source)
+        def _():
+            pltpu.make_async_copy(two(gz, c, zl), two(gx, c, x), gc_r.at[c]).start()
 
     def g_pass(c, d):
-        for b in pair_of(c):
-            pass_line(gz, b, d, gr_s, gl_s, gz_r)
-
-    def x_right(src, o, b, send):
-        return remote(src, blk(xz, b, o), send, xz_r.at[o, b], at_z((z + 1) % 8))
-
-    def x_left(src, o, b, send):
-        return remote(src, blk(xz, b, o), send, xz_r.at[o, b], at_z((z + 7) % 8))
-
-    def transit(b, d):
-        return remote(xc.at[b], xt.at[b], xc_s.at[0, b], xt_r.at[b], at_z((z + d) % 8))
-
-    def x_cross(b):
+        pass_line(gz, c, d, gr_s, gl_s, gz_r)
+
+    def x_right(src, o, c, send):
+        return remote(src, two(xz, c, o), send, xz_r.at[o, c], at_z((z + 1) % 8))
+
+    def x_left(src, o, c, send):
+        return remote(src, two(xz, c, o), send, xz_r.at[o, c], at_z((z + 7) % 8))
+
+    def transit(c, d):
+        return remote(xc.at[pl.ds(2 * c, 2)], xt.at[pl.ds(2 * c, 2)], xc_s.at[0, c], xt_r.at[c], at_z((z + d) % 8))
+
+    def x_cross(c):
         @pl.when(zl == 3)
         def _():
-            x_right(xc.at[b], 3, b, xc_s.at[0, b]).start()
+            x_right(xc.at[pl.ds(2 * c, 2)], 3, c, xc_s.at[0, c]).start()
 
         @pl.when(zl == 0)
         def _():
-            x_left(xc.at[b], 0, b, xc_s.at[0, b]).start()
+            x_left(xc.at[pl.ds(2 * c, 2)], 0, c, xc_s.at[0, c]).start()
 
         @pl.when(zl == 2)
         def _():
-            transit(b, 1).start()
+            transit(c, 1).start()
 
         @pl.when(zl == 1)
         def _():
-            transit(b, 7).start()
-
-    def x_transit(b):
+            transit(c, 7).start()
+
+    def x_transit(c):
         @pl.when(zl == 3)
         def _():
-            transit(b, 1).wait_recv()
-            x_right(xt.at[b], 2, b, xc_s.at[1, b]).start()
+            transit(c, 1).wait_recv()
+            x_right(xt.at[pl.ds(2 * c, 2)], 2, c, xc_s.at[1, c]).start()
 
         @pl.when(zl == 0)
         def _():
-            transit(b, 7).wait_recv()
-            x_left(xt.at[b], 1, b, xc_s.at[1, b]).start()
+            transit(c, 7).wait_recv()
+            x_left(xt.at[pl.ds(2 * c, 2)], 1, c, xc_s.at[1, c]).start()
 
     def x_own(c):
         @pl.when(source)
         def _():
             for b in pair_of(c):
                 pltpu.make_async_copy(x_ref.at[0], blk(xz, b, zl), xa_r.at[b]).wait()
-                own_line(xz, b, xr_s, xl_s, xz_r)
-
-    def x_arrive(b, o, to_right):
+            own_line(xz, c, xr_s, xl_s, xz_r)
+
+    def x_arrive(c, o, to_right):
         if to_right:
-            x_right(blk(xz, b, o), o, b, xr_s.at[o, b]).wait_recv()
+            x_right(two(xz, c, o), o, c, xr_s.at[o, c]).wait_recv()
 
             @pl.when(zl < 3)
             def _():
-                x_right(blk(xz, b, o), o, b, xr_s.at[o, b]).start()
+                x_right(two(xz, c, o), o, c, xr_s.at[o, c]).start()
         else:
-            x_left(blk(xz, b, o), o, b, xl_s.at[o, b]).wait_recv()
+            x_left(two(xz, c, o), o, c, xl_s.at[o, c]).wait_recv()
 
             @pl.when(zl > 0)
             def _():
-                x_left(blk(xz, b, o), o, b, xl_s.at[o, b]).start()
+                x_left(two(xz, c, o), o, c, xl_s.at[o, c]).start()
 
     def x_start(c):
         @pl.when(source)
         def _():
             for b in pair_of(c):
                 pltpu.make_async_copy(x_ref.at[0], xc.at[b], xc_r.at[b]).wait()
-                x_cross(b)
+            x_cross(c)
 
     def x_round(c, hops):
         if hops == 1:
             @pl.when(source)
             def _():
-                for b in pair_of(c):
-                    x_transit(b)
+                x_transit(c)
 
         @pl.when(jnp.logical_not(source))
         def _():
-            for b in pair_of(c):
-                for o, first in ((3, zl + 1), (2, zl + 2), (0, 4 - zl), (1, 5 - zl)):
-                    @pl.when(first == hops)
-                    def _():
-                        x_arrive(b, o, o >= 2)
+            for o, first in ((3, zl + 1), (2, zl + 2), (0, 4 - zl), (1, 5 - zl)):
+                @pl.when(first == hops)
+                def _():
+                    x_arrive(c, o, o >= 2)
 
     def x_pass(c, d):
         @pl.when(source)
         def _():
-            for b in pair_of(c):
-                pass_line(xz, b, d, xr_s, xl_s, xz_r)
+            pass_line(xz, c, d, xr_s, xl_s, xz_r)
+
+    def g_cross(near, c):
+        o = jnp.where(zl == 3, near, 3 - near)
+        return remote(two(gz, c, o), two(gx, c, x), gc_s.at[near, c], gc_r.at[c], dev(1 - zh, y, zh, x, o))
+
+    def g_over(c):
+        @pl.when(at_end)
+        def _():
+            g_cross(0, c).start()
+            g_cross(1, c).start()
 
     def ring_own(c):
-        for b in pair_of(c):
-            pltpu.make_async_copy(g_ref.at[0], blk(gx, b, x), ga_r.at[b]).wait()
-            ring_right(x, b).start()
-            ring_left(x, b).start()
+        pltpu.make_async_copy(two(gz, c, zl), two(gx, c, x), gc_r.at[c]).wait()
+        ring_right(x, c).start()
+        ring_left(x, c).start()
 
     def ring_pass(c):
         even, odd = pair_of(c)
-        for b in (even, odd):
-            ring_right((x + 3) % 4, b).wait_recv()
-            ring_left((x + 1) % 4, b).wait_recv()
+        ring_right((x + 3) % 4, c).wait_recv()
+        ring_left((x + 1) % 4, c).wait_recv()
         ring_far(True, even).start()
         ring_far(False, odd).start()
 
@@ -369,7 +362,7 @@
 
     def home(b):
         y_, k_ = b // 2, b % 2
-        return remote(fin.at[b], ret.at[degree], rt_s.at[b], rt_r.at[degree], dev(zh, y_, k_, x, zl))
+        return remote(fin.at[b], back_ref.at[degree], rt_s.at[b], rt_r.at[degree], dev(zh, y_, k_, x, zl))
 
     def back_reduce(c):
         for way in (0, 1):
@@ -379,7 +372,7 @@
 
             @pl.when(b == me)
             def _():
-                pltpu.make_async_copy(fin.at[b], ret.at[degree], rt_r.at[degree]).start()
+                pltpu.make_async_copy(fin.at[b], back_ref.at[degree], rt_r.at[degree]).start()
 
             @pl.when(b != me)
             def _():
@@ -415,7 +408,7 @@
 
     def wgrad_to(d, o):
         return remote(
-            acc.at[k, o, :, lanes((x + d) % 4)], wg.at[k, owner_rows(o)],
+            acc.at[k, o, :, lanes((x + d) % 4)], wgrad_ref.at[k, owner_rows(o)],
             wo_s.at[d, o], wo_r.at[x % 2, k, o], dev(zh, y, x // 2, (x + d) % 4, zl),
         )
 
@@ -438,7 +431,7 @@
         @pl.when(k == x // 2)
         def _():
             pltpu.make_async_copy(
-                acc.at[k, o, :, lanes(x)], wg.at[k, owner_rows(o)], wo_r.at[x % 2, k, o]
+                acc.at[k, o, :, lanes(x)], wgrad_ref.at[k, owner_rows(o)], wo_r.at[x % 2, k, o]
             ).start()
 
         @pl.when(k != x // 2)
@@ -455,9 +448,18 @@
         when_chunk(s, x_start)
         when_chunk(s - 1, lambda c: g_pass(c, 1))
         when_chunk(s - 1, lambda c: x_round(c, 1))
-        when_chunk(s - 1, ring_own)
+
+        @pl.when(source)
+        def _():
+            when_chunk(s - 1, ring_own)
+
         when_chunk(s - 2, lambda c: g_pass(c, 2))
         when_chunk(s - 2, lambda c: x_round(c, 2))
+
+        @pl.when(source)
+        def _():
+            when_chunk(s - 2, ring_pass)
+
 
         @pl.when(s == 3)
         def _():
@@ -467,17 +469,26 @@
 
         def product(c):
             g_pass(c, 3)
+            g_over(c)
             back_product(c)
 
         when_chunk(s - 3, product)
         when_chunk(s - 3, x_own)
         when_chunk(s - 3, lambda c: x_round(c, 3))
-        when_chunk(s - 2, ring_pass)
         when_chunk(s - 4, back_relay)
         when_chunk(s - 4, lambda c: x_round(c, 4))
-        when_chunk(s - 3, ring_end)
+        @pl.when(source)
+        def _():
+            when_chunk(s - 3, ring_end)
+
+        @pl.when(jnp.logical_not(source))
+        def _():
+            when_chunk(s - 4, ring_own)
+            when_chunk(s - 5, ring_pass)
+            when_chunk(s - 6, ring_end)
+
         when_chunk(s - 5, lambda c: x_round(c, 5))
-        when_chunk(s - 5, back_reduce)
+        when_chunk(s - 6, back_reduce)
         return 0
 
     def every(work):
@@ -492,48 +503,40 @@
     x_round(2, 5)
     x_round(3, 5)
     every(lambda c: x_pass(c, 1))
+
+    @pl.when(jnp.logical_not(source))
+    def _():
+        ring_own(3)
+        ring_pass(2)
+        ring_end(1)
+        ring_pass(3)
+        ring_end(2)
+        ring_end(3)
+
     back_relay(3)
+    back_reduce(1)
     wgrad_product(0)
-    back_reduce(2)
     wgrad_product(1)
     wgrad_send(0)
     every(lambda c: x_pass(c, 2))
+    back_reduce(2)
     wgrad_product(2)
     wgrad_send(1)
-    back_reduce(3)
     every(lambda c: x_pass(c, 3))
     wgrad_product(3)
     wgrad_send(2)
     wgrad_send(3)
-
-    def returned(l, _):
-        pltpu.make_async_copy(fin.at[0], ret.at[l], rt_r.at[l]).wait()
-        return 0
-
-    lax.fori_loop(0, NB, returned, 0)
-    back_out = pltpu.make_async_copy(ret, back_ref, out_s.at[1])
-    back_out.start()
-
-    def owned(o, _):
-        for r in range(2):
-            for k_ in range(2):
-                at = pl.ds(pl.multiple_of(r * 512 + o * 128, 128), 128)
-                pltpu.make_async_copy(acc.at[0, 0, :, pl.ds(0, 128)], wg.at[k_, at], wo_r.at[r, k_, o]).wait()
-        return 0
-
-    lax.fori_loop(0, NZ, owned, 0)
-    wg_out = pltpu.make_async_copy(wg, wgrad_ref, out_s.at[0])
-    wg_out.start()
-
-    def drain(b, _):
-        @pl.when(source)
-        def _():
-            drain_line(xz, b, xr_s, xl_s, xz_r)
-            x_right(xc.at[b], 3, b, xc_s.at[0, b]).wait_send()
+    back_reduce(3)
+
+    def drain_pairs(c, _):
+        @pl.when(source)
+        def _():
+            drain_line(xz, c, xr_s, xl_s, xz_r)
+            x_right(xc.at[pl.ds(2 * c, 2)], 3, c, xc_s.at[0, c]).wait_send()
 
             @pl.when((zl == 0) | (zl == 3))
             def _():
-                x_right(xt.at[b], 2, b, xc_s.at[1, b]).wait_send()
+                x_right(xt.at[pl.ds(2 * c, 2)], 2, c, xc_s.at[1, c]).wait_send()
 
         @pl.when(jnp.logical_not(source))
         def _():
@@ -541,19 +544,26 @@
                 if o >= 2:
                     @pl.when(zl < 3)
                     def _():
-                        x_right(blk(xz, b, o), o, b, xr_s.at[o, b]).wait_send()
+                        x_right(two(xz, c, o), o, c, xr_s.at[o, c]).wait_send()
                 else:
                     @pl.when(zl > 0)
                     def _():
-                        x_left(blk(xz, b, o), o, b, xl_s.at[o, b]).wait_send()
-
-        drain_line(gz, b, gr_s, gl_s, gz_r)
-        for send in (0, 1, 2):
-            remote(blk(gx, b, x), blk(gx, b, x), gx_s.at[send, b], gx_r.at[0, b], dev(zh, y, 1 - k, x, zl)).wait_send()
-
-        @pl.when(jnp.logical_or(zh != k, b != zh * 4 + y))
-        def _():
-            pltpu.make_async_copy(g_ref.at[b], blk(gx, 0, x), ga_s.at[b]).wait()
+                        x_left(two(xz, c, o), o, c, xl_s.at[o, c]).wait_send()
+
+        drain_line(gz, c, gr_s, gl_s, gz_r)
+        @pl.when(at_end)
+        def _():
+            g_cross(0, c).wait_send()
+            g_cross(1, c).wait_send()
+
+        ring_right(x, c).wait_send()
+        ring_left(x, c).wait_send()
+        return 0
+
+    lax.fori_loop(0, 4, drain_pairs, 0)
+
+    def drain(b, _):
+        ring_far(True, b).wait_send()
 
         @pl.when(jnp.logical_or(zh != k, b % 4 != y))
         def _():
@@ -578,7 +588,13 @@
     for copy in w_copies:
         copy.wait_send()
 
-    def drain_wgrad(o, _):
+    def returned(l, _):
+        pltpu.make_async_copy(fin.at[0], back_ref.at[l], rt_r.at[l]).wait()
+        return 0
+
+    lax.fori_loop(0, NB, returned, 0)
+
+    def owned(o, _):
         swap(o).wait_send()
         for d in (1, 2, 3):
             wgrad_to(d, o).wait_send()
@@ -587,12 +603,13 @@
         def _():
             wgrad_to(0, o).wait_send()
 
-        return 0
-
-    lax.fori_loop(0, NZ, drain_wgrad, 0)
-
-    wg_out.wait()
-    back_out.wait()
+        for r in range(2):
+            for k_ in range(2):
+                at = pl.ds(pl.multiple_of(r * 512 + o * 128, 128), 128)
+                pltpu.make_async_copy(acc.at[0, 0, :, pl.ds(0, 128)], wgrad_ref.at[k_, at], wo_r.at[r, k_, o]).wait()
+        return 0
+
+    lax.fori_loop(0, NZ, owned, 0)
 
 
 def per_device(window, inputs, out_grad, weights):
@@ -634,12 +651,10 @@
             vmem((2, NB, half, 128), F32),
             vmem((2, NB, rows, 128), F32),
             vmem((NB, rows, 128), F32),
-            vmem((NB, rows, 128), F32),
-            vmem((2, 1024, 128), F32),
-            dma((8,)), dma((8,)), dma((8,)), dma((2, 8)), dma((8,)),
-            dma((8,)), dma((8,)), dma((8,)), dma((8,)), dma((4,)), dma((4,)), dma(()),
-            dma((4, 8)), dma((4, 8)), dma((4, 8)), dma((4, 8)), dma((4, 8)), dma((4, 8)), dma((3, 8)), dma((3, 8)),
-            dma((4,)), dma((4,)), dma((4, 4)), dma((2, 2, 4)), dma((2, 4)), dma((2, 4)), dma((2, 4)), dma((2, 4)), dma((8,)), dma((8,)), dma((2,)), dma((2,)),
+            dma((8,)), dma((8,)), dma((8,)), dma((2, 4)), dma((4,)),
+            dma((2, 4)), dma((4,)), dma((8,)), dma((8,)), dma((4,)), dma((4,)), dma(()),
+            dma((4, 4)), dma((4, 4)), dma((4, 4)), dma((4, 4)), dma((4, 4)), dma((4, 4)), dma((3, 8)), dma((3, 8)),
+            dma((4,)), dma((4,)), dma((4, 4)), dma((2, 2, 4)), dma((2, 4)), dma((2, 4)), dma((2, 4)), dma((2, 4)), dma((8,)), dma((8,)), dma((2,)),
         ],
         compiler_params=pltpu.CompilerParams(
             collective_id=0, has_side_effects=True, vmem_limit_bytes=44 * 2**20

time: 106 us -> 100 us (0.943)
  Pallas kernels: 99.9 us -> 94.5 us
    pallas_call x1, Pallas kernels: 99.9 us -> 94.5 us  [per_device(): pl.pallas_call(functools.partial(kernel, orders, rows), name='mix_back',...]
where the time goes in v5:
time: 100 us
  Pallas kernels  94.5 us (94%)
  local copies, waits for them, and re-layouts  4.23 us (4%)
  between operations  1.29 us (1%)
    pallas_call x1, Pallas kernels, per_device(): pl.pallas_call(functools.partial(kernel, orders, rows), name='mix_back',...  94.5 us
    unnamed x6, local copies, waits for them, and re-layouts  4.23 us

profile of v5, /device:TPU:1, one launch (start us, length us, event | category | flops | bytes accessed | tf_op | source)
XLA Modules:
  0.0 100.0 jit_solution(10249309234270063963)
XLA Ops:
  1.3 0.0 copy-start
  1.3 1.0 copy-done
  2.3 0.0 copy-start.1
  2.3 1.0 copy-done.1
  3.3 94.5 %mix_back.1 = (f32[8,192,128]{2,1,0:T(8,128)S(1)}, f32[2,1024,128]{2,1,0:T(8,128)S(1)}) custom-call(s32[1]{0:T(128)S(6)} %copy.11.window_ref, bf16[2,2,45,8,128]{4,3,2,1,0:T(8,128)(2,1)S(1)} %bitcast.9, bf16[2,2,45,8,128]{4,3,2,1,0:T(8,128)(2,1)S(1)} %bitcast.10, bf16[2,8,4,4,128,128]{5,4,3,2,1,0:T(8,128)(2,1)} %bitcast.11), custom_call_target="tpu_custom_call" | custom-call | tf_op jit(solution)/shard_map/mix_back/pallas_call | solution.py:622
  97.8 1.3 %copy.9 = f32[8,2,2,45,128]{4,0,3,2,1:T(8,128)} copy(f32[8,2,2,45,128]{4,3,2,1,0:T(8,128)S(1)} %bitcast.8) | data formatting | bytes 1474560
  99.0 1.0 copy.12
Async XLA Ops:
  1.3 1.0 copy-start
  2.3 1.0 copy-start.1

commit v6 on v5

--- a/solution.py
+++ b/solution.py
@@ -118,29 +118,6 @@
     lax.fori_loop(1, 8, gi_step, 0)
     degree = 4 * k + y
     pltpu.make_async_copy(g_ref.at[degree], blk(gz, me, zl), gi_r.at[me]).start()
-    source = zh == k
-
-    def x_out(t, _):
-        y_ = (y + t) % 4
-        mine, other = zh * 4 + y_, (1 - zh) * 4 + y_
-        itself = jnp.logical_and(source, t == 0)
-
-        @pl.when(itself)
-        def _():
-            pltpu.make_async_copy(x_ref.at[mine], blk(xz, me, zl), xa_r.at[me]).start()
-            pltpu.make_async_copy(x_ref.at[other], xc.at[me], xc_r.at[me]).start()
-
-        @pl.when(jnp.logical_not(itself))
-        def _():
-            to = dev(zh, y_, zh, x, zl)
-            remote(x_ref.at[mine], blk(xz, me, zl), xa_s.at[mine], xa_r.at[me], to).start()
-            remote(x_ref.at[other], xc.at[me], xa_s.at[other], xc_r.at[me], to).start()
-
-        return 0
-
-    lax.fori_loop(0, 4, x_out, 0)
-
-
     w_loc_copy = pltpu.make_async_copy(w_ref.at[:, degree, :, zl], wt.at[:, :, :, lanes(zl)], w_loc)
     w_loc_copy.start()
     w_copies = []
@@ -151,6 +128,29 @@
             remote(w_ref.at[reim, degree, :, to % 4], wt.at[reim, :, :, lanes(zl)], w_s.at[i], w_r.at[i], at_z(to))
         )
         w_copies[-1].start()
+
+    source = zh == k
+
+    def x_out(t, _):
+        y_ = (y + t) % 4
+        mine, other = zh * 4 + y_, (1 - zh) * 4 + y_
+        itself = jnp.logical_and(source, t == 0)
+
+        @pl.when(itself)
+        def _():
+            pltpu.make_async_copy(x_ref.at[mine], blk(xz, me, zl), xa_r.at[me]).start()
+            pltpu.make_async_copy(x_ref.at[other], xc.at[me], xc_r.at[me]).start()
+
+        @pl.when(jnp.logical_not(itself))
+        def _():
+            to = dev(zh, y_, zh, x, zl)
+            remote(x_ref.at[mine], blk(xz, me, zl), xa_s.at[mine], xa_r.at[me], to).start()
+            remote(x_ref.at[other], xc.at[me], xa_s.at[other], xc_r.at[me], to).start()
+
+        return 0
+
+    lax.fori_loop(0, 4, x_out, 0)
+
 
     def right(buf, o, c, send, recv):
         return remote(two(buf, c, o), two(buf, c, o), send.at[o, c], recv.at[o, c], dev(zh, y, k, x, (zl + 1) % 4))
@@ -445,16 +445,16 @@
 
     def pipeline(s, _):
         when_chunk(s, g_own)
-        when_chunk(s, x_start)
+        when_chunk(s - 1, x_start)
         when_chunk(s - 1, lambda c: g_pass(c, 1))
-        when_chunk(s - 1, lambda c: x_round(c, 1))
+        when_chunk(s - 2, lambda c: x_round(c, 1))
 
         @pl.when(source)
         def _():
             when_chunk(s - 1, ring_own)
 
         when_chunk(s - 2, lambda c: g_pass(c, 2))
-        when_chunk(s - 2, lambda c: x_round(c, 2))
+        when_chunk(s - 3, lambda c: x_round(c, 2))
 
         @pl.when(source)
         def _():
@@ -472,11 +472,11 @@
             g_over(c)
             back_product(c)
 
+        when_chunk(s - 4, back_relay)
         when_chunk(s - 3, product)
         when_chunk(s - 3, x_own)
-        when_chunk(s - 3, lambda c: x_round(c, 3))
-        when_chunk(s - 4, back_relay)
-        when_chunk(s - 4, lambda c: x_round(c, 4))
+        when_chunk(s - 4, lambda c: x_round(c, 3))
+        when_chunk(s - 5, lambda c: x_round(c, 4))
         @pl.when(source)
         def _():
             when_chunk(s - 3, ring_end)
@@ -487,7 +487,7 @@
             when_chunk(s - 5, ring_pass)
             when_chunk(s - 6, ring_end)
 
-        when_chunk(s - 5, lambda c: x_round(c, 5))
+        when_chunk(s - 6, lambda c: x_round(c, 5))
         when_chunk(s - 6, back_reduce)
         return 0
 
@@ -499,6 +499,15 @@
         lax.fori_loop(0, 4, step, 0)
 
     lax.fori_loop(0, 7, pipeline, 0)
+    x_round(3, 3)
+    x_round(2, 4)
+    x_round(1, 5)
+
+    @pl.when(jnp.logical_not(source))
+    def _():
+        ring_own(3)
+
+    back_relay(3)
     x_round(3, 4)
     x_round(2, 5)
     x_round(3, 5)
@@ -506,22 +515,20 @@
 
     @pl.when(jnp.logical_not(source))
     def _():
-        ring_own(3)
         ring_pass(2)
         ring_end(1)
         ring_pass(3)
         ring_end(2)
         ring_end(3)
 
-    back_relay(3)
+    every(lambda c: x_pass(c, 2))
     back_reduce(1)
     wgrad_product(0)
     wgrad_product(1)
     wgrad_send(0)
-    every(lambda c: x_pass(c, 2))
-    back_reduce(2)
     wgrad_product(2)
     wgrad_send(1)
+    back_reduce(2)
     every(lambda c: x_pass(c, 3))
     wgrad_product(3)
     wgrad_send(2)

time: 100 us -> 97.2 us (0.972)
  Pallas kernels: 94.5 us -> 91.6 us
    pallas_call x1, Pallas kernels: 94.5 us -> 91.6 us  [per_device(): pl.pallas_call(functools.partial(kernel, orders, rows), name='mix_back',...]
where the time goes in v6:
time: 97.2 us; the launch traced here: 97.1 us
  Pallas kernels  91.6 us (94%)
  local copies, waits for them, and re-layouts  4.23 us (4%)
  between operations  1.29 us (1%)
    pallas_call x1, Pallas kernels, per_device(): pl.pallas_call(functools.partial(kernel, orders, rows), name='mix_back',...  91.6 us
    unnamed x6, local copies, waits for them, and re-layouts  4.23 us

profile of v6, /device:TPU:1, one launch (start us, length us, event | category | flops | bytes accessed | tf_op | source)
XLA Modules:
  0.0 97.1 jit_solution(16136562192354035494)
XLA Ops:
  1.3 0.0 copy-start
  1.3 1.0 %copy-done = bf16[2,2,8,45,128]{4,2,3,1,0:T(8,128)(2,1)S(1)} copy-done((bf16[2,2,8,45,128]{4,2,3,1,0:T(8,128)(2,1)S(1)}, bf16[2,2,8,45,128]{4,2,3,1,0:T(8,128)(2,1)}, u32[]{:S(2)}) %copy-start) | copy-done | bytes 368664
  2.3 0.0 copy-start.1
  2.3 1.0 %copy-done.1 = bf16[2,2,8,45,128]{4,2,3,1,0:T(8,128)(2,1)S(1)} copy-done((bf16[2,2,8,45,128]{4,2,3,1,0:T(8,128)(2,1)S(1)}, bf16[2,2,8,45,128]{4,2,3,1,0:T(8,128)(2,1)}, u32[]{:S(2)}) %copy-start.1) | copy-done | bytes 368664
  3.3 91.6 %mix_back.1 = (f32[8,192,128]{2,1,0:T(8,128)S(1)}, f32[2,1024,128]{2,1,0:T(8,128)S(1)}) custom-call(s32[1]{0:T(128)S(6)} %copy.11.window_ref, bf16[2,2,45,8,128]{4,3,2,1,0:T(8,128)(2,1)S(1)} %bitcast.9, bf16[2,2,45,8,128]{4,3,2,1,0:T(8,128)(2,1)S(1)} %bitcast.10, bf16[2,8,4,4,128,128]{5,4,3,2,1,0:T(8,128)(2,1)} %bitcast.11), custom_call_target="tpu_custom_call" | custom-call | tf_op jit(solution)/shard_map/mix_back/pallas_call | solution.py:629
  94.8 1.3 %copy.9 = f32[8,2,2,45,128]{4,0,3,2,1:T(8,128)} copy(f32[8,2,2,45,128]{4,3,2,1,0:T(8,128)S(1)} %bitcast.8) | data formatting | bytes 1474560
  96.1 1.0 copy.12
Async XLA Ops:
  1.3 1.0 %copy-start = (bf16[2,2,8,45,128]{4,2,3,1,0:T(8,128)(2,1)S(1)}, bf16[2,2,8,45,128]{4,2,3,1,0:T(8,128)(2,1)}, u32[]{:S(2)}) copy-start(bf16[2,2,8,45,128]{4,2,3,1,0:T(8,128)(2,1)} %param.5) | copy-start | bytes 1105924
  2.3 1.0 %copy-start.1 = (bf16[2,2,8,45,128]{4,2,3,1,0:T(8,128)(2,1)S(1)}, bf16[2,2,8,45,128]{4,2,3,1,0:T(8,128)(2,1)}, u32[]{:S(2)}) copy-start(bf16[2,2,8,45,128]{4,2,3,1,0:T(8,128)(2,1)} %param.6) | copy-start | bytes 1105924

commit v7 on v6

--- a/solution.py
+++ b/solution.py
@@ -28,7 +28,7 @@
     x_in, g_in, x_ref, g_ref, xz, xc, xt, gx, gp, gz, wt, acc, pair, part, relay, heap, fin,
     xa_s, xa_r, xc_r, xc_s, xt_r, gc_s, gc_r, gi_s, gi_r, w_s, w_r, w_loc,
     xr_s, xl_s, xz_r, gr_s, gl_s, gz_r, gx_s, gx_r,
-    pair_s, pair_r, wo_s, wo_r, far_s, far_r, rs_s, rs_r, rt_s, rt_r, in_s,
+    pair_s, pair_r, wo_s, wo_r, far_s, far_r, np_s, np_r, rs_s, rs_r, rt_s, rt_r, in_s,
 ):
     zh, y, k, x, zl = coords()
     z = zh * 4 + zl
@@ -342,10 +342,12 @@
             dev(zh, y, k, (x + 1 + 2 * way) % 4, zl),
         )
 
-    def near(way, c):
+    def near(way, c, added):
         x_ = (x + 1 + 2 * way) % 4
+        at = pl.ds(0, half) if (way == 0) == added else pl.ds(half, half)
+        send, recv = (rs_s, rs_r) if added else (np_s, np_r)
         return remote(
-            part.at[x_, pl.ds(2 * c, 2)], heap.at[way, pl.ds(2 * c, 2)], rs_s.at[way, c], rs_r.at[way, c],
+            part.at[x_, pl.ds(2 * c, 2), at], heap.at[way, pl.ds(2 * c, 2), at], send.at[way, c], recv.at[way, c],
             dev(zh, y, k, x_, zl),
         )
 
@@ -358,7 +360,7 @@
                     part[x_, b, 0:half] = part[x_, b, 0:half] + relay[way, b]
                 else:
                     part[x_, b, half:rows] = part[x_, b, half:rows] + relay[way, b]
-            near(way, c).start()
+            near(way, c, True).start()
 
     def home(b):
         y_, k_ = b // 2, b % 2
@@ -366,7 +368,8 @@
 
     def back_reduce(c):
         for way in (0, 1):
-            near(way, c).wait_recv()
+            near(way, c, False).wait_recv()
+            near(way, c, True).wait_recv()
         for b in pair_of(c):
             fin[b] = part[x, b] + (heap[0, b] + heap[1, b])
 
@@ -392,6 +395,8 @@
                 part[x_, 2 * c + j, half:rows] = back_im[:, x_ * 128 : (x_ + 1) * 128]
         for way in (0, 1):
             far(way, c).start()
+        for way in (0, 1):
+            near(way, c, False).start()
 
     def nth(t):
         if t == 0:
@@ -512,6 +517,7 @@
     x_round(2, 5)
     x_round(3, 5)
     every(lambda c: x_pass(c, 1))
+    every(lambda c: x_pass(c, 2))
 
     @pl.when(jnp.logical_not(source))
     def _():
@@ -521,9 +527,8 @@
         ring_end(2)
         ring_end(3)
 
-    every(lambda c: x_pass(c, 2))
+    wgrad_product(0)
     back_reduce(1)
-    wgrad_product(0)
     wgrad_product(1)
     wgrad_send(0)
     wgrad_product(2)
@@ -588,7 +593,8 @@
     def drain_scatter(c, _):
         for way in (0, 1):
             far(way, c).wait_send()
-            near(way, c).wait_send()
+            near(way, c, False).wait_send()
+            near(way, c, True).wait_send()
         return 0
 
     lax.fori_loop(0, NB // 2, drain_scatter, 0)
@@ -661,7 +667,7 @@
             dma((8,)), dma((8,)), dma((8,)), dma((2, 4)), dma((4,)),
             dma((2, 4)), dma((4,)), dma((8,)), dma((8,)), dma((4,)), dma((4,)), dma(()),
             dma((4, 4)), dma((4, 4)), dma((4, 4)), dma((4, 4)), dma((4, 4)), dma((4, 4)), dma((3, 8)), dma((3, 8)),
-            dma((4,)), dma((4,)), dma((4, 4)), dma((2, 2, 4)), dma((2, 4)), dma((2, 4)), dma((2, 4)), dma((2, 4)), dma((8,)), dma((8,)), dma((2,)),
+            dma((4,)), dma((4,)), dma((4, 4)), dma((2, 2, 4)), dma((2, 4)), dma((2, 4)), dma((2, 4)), dma((2, 4)), dma((2, 4)), dma((2, 4)), dma((8,)), dma((8,)), dma((2,)),
         ],
         compiler_params=pltpu.CompilerParams(
             collective_id=0, has_side_effects=True, vmem_limit_bytes=44 * 2**20

time: 97.2 us -> 96.8 us (level)
  no operation moved by 1% of the time
where the time goes in v7:
time: 96.8 us; the launch traced here: 96.6 us
  Pallas kernels  91.1 us (94%)
  local copies, waits for them, and re-layouts  4.23 us (4%)
  between operations  1.29 us (1%)
    pallas_call x1, Pallas kernels, per_device(): pl.pallas_call(functools.partial(kernel, orders, rows), name='mix_back',...  91.1 us
    unnamed x6, local copies, waits for them, and re-layouts  4.23 us

profile of v7, /device:TPU:1, one launch (start us, length us, event | category | flops | bytes accessed | tf_op | source)
XLA Modules:
  0.0 96.6 jit_solution(15225321601136192648)
XLA Ops:
  1.3 0.0 copy-start
  1.3 1.0 %copy-done = bf16[2,2,8,45,128]{4,2,3,1,0:T(8,128)(2,1)S(1)} copy-done((bf16[2,2,8,45,128]{4,2,3,1,0:T(8,128)(2,1)S(1)}, bf16[2,2,8,45,128]{4,2,3,1,0:T(8,128)(2,1)}, u32[]{:S(2)}) %copy-start) | copy-done | bytes 368664
  2.3 0.0 copy-start.1
  2.3 1.0 %copy-done.1 = bf16[2,2,8,45,128]{4,2,3,1,0:T(8,128)(2,1)S(1)} copy-done((bf16[2,2,8,45,128]{4,2,3,1,0:T(8,128)(2,1)S(1)}, bf16[2,2,8,45,128]{4,2,3,1,0:T(8,128)(2,1)}, u32[]{:S(2)}) %copy-start.1) | copy-done | bytes 368664
  3.3 91.1 %mix_back.1 = (f32[8,192,128]{2,1,0:T(8,128)S(1)}, f32[2,1024,128]{2,1,0:T(8,128)S(1)}) custom-call(s32[1]{0:T(128)S(6)} %copy.11.window_ref, bf16[2,2,45,8,128]{4,3,2,1,0:T(8,128)(2,1)S(1)} %bitcast.9, bf16[2,2,45,8,128]{4,3,2,1,0:T(8,128)(2,1)S(1)} %bitcast.10, bf16[2,8,4,4,128,128]{5,4,3,2,1,0:T(8,128)(2,1)} %bitcast.11), custom_call_target="tpu_custom_call" | custom-call | tf_op jit(solution)/shard_map/mix_back/pallas_call | solution.py:635
  94.3 1.3 %copy.9 = f32[8,2,2,45,128]{4,0,3,2,1:T(8,128)} copy(f32[8,2,2,45,128]{4,3,2,1,0:T(8,128)S(1)} %bitcast.8) | data formatting | bytes 1474560
  95.6 1.0 %copy.12 = f32[2,1024,128]{2,1,0:T(8,128)} copy(f32[2,1024,128]{2,1,0:T(8,128)S(1)} %get-tuple-element.9) | data formatting | bytes 2097152
Async XLA Ops:
  1.3 1.0 %copy-start = (bf16[2,2,8,45,128]{4,2,3,1,0:T(8,128)(2,1)S(1)}, bf16[2,2,8,45,128]{4,2,3,1,0:T(8,128)(2,1)}, u32[]{:S(2)}) copy-start(bf16[2,2,8,45,128]{4,2,3,1,0:T(8,128)(2,1)} %param.5) | copy-start | bytes 1105924
  2.3 1.0 %copy-start.1 = (bf16[2,2,8,45,128]{4,2,3,1,0:T(8,128)(2,1)S(1)}, bf16[2,2,8,45,128]{4,2,3,1,0:T(8,128)(2,1)}, u32[]{:S(2)}) copy-start(bf16[2,2,8,45,128]{4,2,3,1,0:T(8,128)(2,1)} %param.6) | copy-start | bytes 1105924
